TPU v7x, 256 devices: a whole 4x4x8 slice. The times are simulated.
256 devices in a mesh: gx: 16 (over y, x), gy: 8 (over z_lo, core), gz: 2 (over z_hi).
Axes of the slice: x: 4, y: 4, z: 8 (z_hi: 2, z_lo: 4; z = z_hi * 4 + z_lo), core: 2. Of those that a mesh axis runs over, the one named last changes fastest.
Arguments:
- adjoint_source: float32 [2, 128, 256, 256], P(None, 'gx', 'gy', 'gz'), may hold values from -6 to 6
- velocity: float32 [128, 256, 256], P('gx', 'gy', 'gz'), may hold values from 1.5 to 4.5
- damping: float32 [128, 256, 256], P('gx', 'gy', 'gz'), may hold values from 0.02 to 0.6
- face_rounds: int32 [16, 8, 2, 6], P('gx', 'gy', 'gz'), may hold values from 0 to 5, as said below
- aggregates: int32 [32, 32, 2], P('gx', 'gy', 'gz'), may hold values from 0 to 511, as said below
Outputs:
- adjoint_field: float32 [2, 128, 256, 256], P(None, 'gx', 'gy', 'gz')
Inputs may be any that keep to these rules, and one draw needn't show every extreme that they name: `face_rounds`: entry k of subdomain (i, j, l) is the round of its k-th face in the order low first dimension, high first dimension, low second, high second, low depth, high depth. Two subdomains that share a face give it the same round, the six faces of a subdomain have six different rounds, and the faces along one dimension use the same two rounds in every subdomain. Faces on the grid's outer boundary carry a round too. `aggregates`: every aggregate holds exactly 4 coarse cells.
All inputs are finite; a program needn't handle non-finite values.
Results may differ from a plain program's by a relative error of at most 0.0003.
Values sent between devices are 32-bit elements; how exact they have to be, the bound alone decides.
A program may use at most 128 MiB of HBM per device.

v0:
```python
import functools

import jax
import jax.numpy as jnp
from jax import lax
from jax.experimental import pallas as pl
from jax.experimental.pallas import tpu as pltpu
from jax.sharding import PartitionSpec as P

MESH = pl.DeviceIdType.MESH
F32 = jnp.float32
BF16 = jnp.bfloat16

CX, CY, CZ = 8, 32, 128
PY = 48
TILES = CY // 8
SWEEPS = 3
SMOOTH = 4
GAMMA_RE = 0.6
GAMMA_IM = 0.25
RELAX = 0.8
OMEGA_SQ = 9.0

OFFSETS = [(ox, oy) for ox in (-1, 0, 1) for oy in (-1, 0, 1)]
NEIGHBOURS = [(ox, oy, 1) for ox, oy in OFFSETS if ox and oy]
NEIGHBOURS += [(ox, oy, 1) for ox, oy in OFFSETS if not (ox and oy)]
NEIGHBOURS += [(ox, oy, 0) for ox, oy in OFFSETS if ox and not oy]
NEIGHBOURS += [(ox, oy, 0) for ox, oy in OFFSETS if ox and oy]
NEIGHBOURS += [(ox, oy, 0) for ox, oy in OFFSETS if oy and not ox]


def slot_of(ox, oy):
    return (ox + 1) * 3 + (oy + 1)


def corner_of(ox, oy):
    return (1 if ox > 0 else 0) * 2 + (1 if oy > 0 else 0)


def iota(dim, shape=(8, 128)):
    return lax.broadcasted_iota(jnp.int32, shape, dim)


def roll(v, lanes, subs=0):
    if isinstance(lanes, int):
        lanes = lanes % 128
    if not isinstance(lanes, int) or lanes:
        v = pltpu.roll(v, lanes, 1)
    if subs % 8:
        v = pltpu.roll(v, subs % 8, 0)
    return v


def blend(a, b, mask):
    d_re = b[0] - a[0]
    d_im = b[1] - a[1]
    t_re = GAMMA_RE * d_re - GAMMA_IM * d_im
    t_im = GAMMA_RE * d_im + GAMMA_IM * d_re
    if mask is not None:
        t_re = jnp.where(mask, t_re, 0.0)
        t_im = jnp.where(mask, t_im, 0.0)
    return (a[0] + t_re, a[1] + t_im), (b[0] - t_re, b[1] - t_im)


def kernel(
    nx, ny,
    src, vel, dmp, rounds, aggs, out,
    kap, kdm, mre, mim, res, ping, pong, cor, fld, fz,
    coltile, edgecol, onehot, ktile,
    info_send, info_recv, stage, rz, ry, rd, ar_src1, ar_src2, ar1, ar2,
    info_ss, info_rs, h_ss, h_rs, x_ss, x_rs, ar_ss, ar_rs,
):
    ix, iy, iz = lax.axis_index("gx"), lax.axis_index("gy"), lax.axis_index("gz")
    lane, sub = iota(1), iota(0)
    lx, lt = lane % 8, (lane // 8) % TILES
    zf = jnp.where(iz == 0, 127, 0).astype(jnp.int32)
    at_face = lane == zf
    first_lane, last_lane = lane == 0, lane == 127
    lane32 = iota(1, (32, 128))
    first32, last32 = lane32 == 0, lane32 == 127

    has_x = {-1: ix > 0, 1: ix < nx - 1}
    has_y = {-1: iy > 0, 1: iy < ny - 1}

    def exists(ox, oy):
        if ox and oy:
            return jnp.logical_and(has_x[ox], has_y[oy])
        if ox:
            return has_x[ox]
        if oy:
            return has_y[oy]
        return None

    def guarded(cond, fn):
        if cond is None:
            fn()
        else:
            pl.when(cond)(fn)

    def device(ox, oy, oz):
        return (ix + ox, iy + oy, (1 - iz) if oz else iz)

    group1 = [(lax.rem(ix + d, nx), iy, iz) for d in range(1, nx)]
    here = iz * ny + iy
    group2 = []
    for d in range(1, 2 * ny):
        there = lax.rem(here + d, 2 * ny)
        group2.append((ix, lax.rem(there, ny), there // ny))

    zero = jnp.zeros((8, 128), F32)
    for k in range(SWEEPS):
        for p in range(2):
            for x in range(10):
                tiles = range(6) if x in (0, 9) else (0, 5)
                for t in tiles:
                    cor[k, p, pl.ds(x * PY + 8 * t, 8), :] = zero
        for s in range(2):
            for o in range(9):
                rz[k, s, o] = zero
        for o in range(2):
            for j in range(3):
                ry[k, o, j] = zero
        for o in range(4):
            for j in range(2):
                rd[k, o, j] = zero
    for s in range(2):
        for o in range(9):
            info_recv[s, o] = zero - 1.0

    barrier = pltpu.get_barrier_semaphore()
    count = jnp.int32(nx - 1 + 2 * ny - 1 + 1)
    for ox, oy, oz in NEIGHBOURS:
        def tell(ox=ox, oy=oy, oz=oz):
            pl.semaphore_signal(barrier, inc=1, device_id=device(ox, oy, oz), device_id_type=MESH)
        guarded(exists(ox, oy), tell)
        if exists(ox, oy) is not None:
            count = count + jnp.where(exists(ox, oy), 1, 0)
    for target in group2 + group1:
        pl.semaphore_signal(barrier, inc=1, device_id=target, device_id_type=MESH)

    for buf in (ping, pong):
        for p in range(2):
            for x in range(8):
                buf[p, pl.ds(x * PY, 8), :] = zero
                buf[p, pl.ds(x * PY + 40, 8), :] = zero
    for p in range(2):
        for x in range(10):
            for t in range(6):
                fld[p, pl.ds(x * PY + 8 * t, 8), :] = zero
        for role in range(4):
            fz[role, p] = zero

    for x in range(CX):
        v = vel[x]
        kappa = OMEGA_SQ / (v * v)
        damp = kappa * dmp[x]
        d_re = 14.0 - kappa
        scale = RELAX / (d_re * d_re + damp * damp)
        kap[x] = 16.0 - kappa
        kdm[x] = damp
        mre[x] = d_re * scale
        mim[x] = -damp * scale

    def face(i, inside):
        return jnp.where(inside, rounds[0, 0, 0, i].astype(F32), -1.0)

    low_x, high_x = face(0, ix > 0), face(1, ix < nx - 1)
    low_y, high_y = face(2, iy > 0), face(3, iy < ny - 1)
    depth = jnp.where(iz == 0, rounds[0, 0, 0, 5].astype(F32), rounds[0, 0, 0, 4].astype(F32))
    ids = [[aggs[qx, qy, 0].astype(F32) for qy in range(TILES)] for qx in range(2)]
    info = jnp.where(lx == 0, low_x, jnp.where(lx == 7, high_x, -1.0))
    col_y = jnp.where((lt == 0) & (sub == 0), low_y, jnp.where((lt == TILES - 1) & (sub == 7), high_y, -1.0))
    info = jnp.where(lane >= 32, col_y, info)
    info = jnp.where(lane >= 64, depth, info)
    for qx in range(2):
        for qy in range(TILES):
            info = jnp.where((lane >= 96) & (lx // 4 == qx) & (lt == qy), ids[qx][qy], info)
    info_send[...] = info

    agg_of = ((sub % 4) * 128 + lane).astype(F32)
    low_rows = sub < 4

    def bucket(sums):
        rows = [jnp.sum(sums[p][qx][t], axis=0, keepdims=True) for p in range(2) for qx in range(2) for t in range(TILES)]
        total = jnp.sum(jnp.concatenate(rows, axis=0), axis=1, keepdims=True)
        tile = zero
        for qx in range(2):
            for t in range(TILES):
                q = qx * TILES + t
                s_re = jnp.broadcast_to(total[q:q + 1], (8, 128))
                s_im = jnp.broadcast_to(total[8 + q:9 + q], (8, 128))
                tile = jnp.where(agg_of == ids[qx][t], tile + jnp.where(low_rows, s_re, s_im), tile)
        return tile

    def rows_of(v, t):
        return v[8 * t:8 * t + 8]

    sums = [[[zero] * TILES for _ in range(2)] for _ in range(2)]
    for x in range(CX):
        kappa, damp = 16.0 - kap[x], kdm[x]
        for t in range(TILES):
            sums[0][x // 4][t] = sums[0][x // 4][t] + rows_of(kappa, t)
            sums[1][x // 4][t] = sums[1][x // 4][t] + rows_of(damp, t)
    ar_src1[SWEEPS] = bucket(sums)

    def assemble(tiles, default):
        def pick(parts):
            value = jnp.full((8, 128), default, F32)
            for mask, tile in parts:
                value = jnp.where(mask, tile, value)
            return value
        t0, t3 = (lt == 0) & (sub == 0), (lt == TILES - 1) & (sub == 7)
        x0, x7 = lx == 0, lx == 7
        across_x = pick([(x0, roll(tiles[(-1, 0)], -7)), (x7, roll(tiles[(1, 0)], 7))])
        across_y = pick([(t0, roll(tiles[(0, -1)], -24, 1)), (t3, roll(tiles[(0, 1)], 24, -1))])
        across_xy = pick([
            (x0 & t0, roll(tiles[(-1, -1)], -31, 1)),
            (x0 & t3, roll(tiles[(-1, 1)], 17, -1)),
            (x7 & t0, roll(tiles[(1, -1)], -17, 1)),
            (x7 & t3, roll(tiles[(1, 1)], 31, -1)),
        ])
        return [tiles[(0, 0)], across_x, across_y, across_xy]

    def smooth_z(v):
        return 2.0 * v + jnp.where(first32, 0.0, pltpu.roll(v, 1, 1)) + jnp.where(last32, 0.0, pltpu.roll(v, 127, 1))

    def residual_pass():
        lefts = []
        for p in range(2):
            c0, px, py, pxy = (fz[role, p] for role in range(4))
            t0, t3 = (lt == 0) & (sub == 0), (lt == TILES - 1) & (sub == 7)

            def smooth_y(v, across):
                up = pltpu.roll(v, 1, 0)
                up = jnp.where(sub == 0, roll(up, 8), up)
                up = jnp.where(t0, across, up)
                down = pltpu.roll(v, 7, 0)
                down = jnp.where(sub == 7, roll(down, -8), down)
                down = jnp.where(t3, across, down)
                return up + 2.0 * v + down

            yc, yx = smooth_y(c0, py), smooth_y(px, pxy)
            w = 2.0 * yc + jnp.where(lx == 0, yx, roll(yc, 1)) + jnp.where(lx == 7, yx, roll(yc, -1))
            lefts.append(pltpu.roll(w, zf, 1))
        sums = [[[zero] * TILES for _ in range(2)] for _ in range(2)]
        ys = [[None] * 10 for _ in range(2)]

        def y_smoothed(p, x):
            if ys[p][x] is None:
                base = x * PY
                ys[p][x] = (fld[p, pl.ds(base + 7, 32), :] + fld[p, pl.ds(base + 9, 32), :]
                            + 2.0 * fld[p, pl.ds(base + 8, 32), :])
            return ys[p][x]

        for x in range(CX):
            smoothed = []
            for p in range(2):
                v = y_smoothed(p, x) + 2.0 * y_smoothed(p, x + 1) + y_smoothed(p, x + 2)
                halo = jnp.concatenate([roll(lefts[p], -(8 * t + x)) for t in range(TILES)], axis=0)
                smoothed.append(smooth_z(v) + jnp.where(lane32 == zf, halo, 0.0))
            f_re = fld[0, pl.ds((x + 1) * PY + 8, 32), :]
            f_im = fld[1, pl.ds((x + 1) * PY + 8, 32), :]
            a, b = kap[x], kdm[x]
            r_re = src[0, x] + 0.25 * smoothed[0] - a * f_re + b * f_im
            r_im = src[1, x] + 0.25 * smoothed[1] - a * f_im - b * f_re
            res[0, x] = r_re
            res[1, x] = r_im
            for t in range(TILES):
                sums[0][x // 4][t] = sums[0][x // 4][t] + rows_of(r_re, t)
                sums[1][x // 4][t] = sums[1][x // 4][t] + rows_of(r_im, t)
        return sums

    def first_pass():
        sums = [[[zero] * TILES for _ in range(2)] for _ in range(2)]
        for x in range(CX):
            for p in range(2):
                v = src[p, x]
                res[p, x] = v
                for t in range(TILES):
                    sums[p][x // 4][t] = sums[p][x // 4][t] + rows_of(v, t)
        return sums

    def jacobi(k):
        for x in range(CX):
            a, b = mre[x], mim[x]
            r_re, r_im = res[0, x], res[1, x]
            ping[0, pl.ds(x * PY + 8, 32), :] = a * r_re - b * r_im
            ping[1, pl.ds(x * PY + 8, 32), :] = a * r_im + b * r_re
        buffers = [ping, pong]
        for step in range(1, SMOOTH):
            now, later = buffers[(step - 1) % 2], buffers[step % 2]
            last = step == SMOOTH - 1
            ys = [[None] * CX for _ in range(2)]

            def y_smoothed(p, x):
                if x < 0 or x >= CX:
                    return None
                if ys[p][x] is None:
                    base = x * PY
                    ys[p][x] = (now[p, pl.ds(base + 7, 32), :] + now[p, pl.ds(base + 9, 32), :]
                                + 2.0 * now[p, pl.ds(base + 8, 32), :])
                return ys[p][x]

            for x in range(CX):
                misfit, old = [], []
                for p in range(2):
                    v = 2.0 * y_smoothed(p, x)
                    for near in (y_smoothed(p, x - 1), y_smoothed(p, x + 1)):
                        if near is not None:
                            v = v + near
                    c = now[p, pl.ds(x * PY + 8, 32), :]
                    old.append(c)
                    misfit.append(res[p, x] + 0.25 * smooth_z(v) - 2.0 * c)
                a, b = mre[x], mim[x]
                new_re = 0.2 * old[0] + (a * misfit[0] - b * misfit[1])
                new_im = 0.2 * old[1] + (a * misfit[1] + b * misfit[0])
                if last:
                    cor[k, 0, pl.ds((x + 1) * PY + 8, 32), :] = new_re
                    cor[k, 1, pl.ds((x + 1) * PY + 8, 32), :] = new_im
                else:
                    later[0, pl.ds(x * PY + 8, 32), :] = new_re
                    later[1, pl.ds(x * PY + 8, 32), :] = new_im

    def remote(src_ref, dst_ref, ssem, rsem, target):
        return pltpu.make_async_remote_copy(
            src_ref=src_ref, dst_ref=dst_ref, send_sem=ssem, recv_sem=rsem,
            device_id=target, device_id_type=MESH)

    def halo_copies(k, ox, oy, oz, incoming):
        mine, theirs = oz * 9 + slot_of(ox, oy), oz * 9 + slot_of(-ox, -oy)
        target = device(ox, oy, oz)
        if oz == 0 and ox and oy:
            part = stage.at[k, pl.ds(5, 2)]
            there, at_home = rd.at[k, corner_of(-ox, -oy)], rd.at[k, corner_of(ox, oy)]
        elif oz == 0 and oy:
            part = stage.at[k, pl.ds(0, 3)] if oy < 0 else stage.at[k, pl.ds(2, 3)]
            there, at_home = ry.at[k, 1 if oy < 0 else 0], ry.at[k, 0 if oy < 0 else 1]
        else:
            part = stage.at[k, 2]
            there, at_home = rz.at[k, oz, slot_of(-ox, -oy)], rz.at[k, oz, slot_of(ox, oy)]
        if incoming:
            return remote(part, at_home, h_ss.at[k, mine], h_rs.at[k, mine], target)
        return remote(part, there, h_ss.at[k, mine], h_rs.at[k, theirs], target)

    def plane_copies(k, ox, incoming):
        own, halo = (1, 9) if ox < 0 else (8, 0)
        part = cor.at[k, :, pl.ds(own * PY + 8, 32), :]
        there = cor.at[k, :, pl.ds(halo * PY + 8, 32), :]
        at_home = cor.at[k, :, pl.ds((0 if ox < 0 else 9) * PY + 8, 32), :]
        mine, theirs = (0, 1) if ox < 0 else (1, 0)
        if incoming:
            return remote(part, at_home, x_ss.at[k, mine], x_rs.at[k, mine], device(ox, 0, 0))
        return remote(part, there, x_ss.at[k, mine], x_rs.at[k, theirs], device(ox, 0, 0))

    def for_halo(k, fn, incoming=False):
        for ox, oy, oz in NEIGHBOURS:
            guarded(exists(ox, oy), lambda ox=ox, oy=oy, oz=oz: fn(halo_copies(k, ox, oy, oz, incoming)))
        for ox in (-1, 1):
            guarded(exists(ox, 0), lambda ox=ox: fn(plane_copies(k, ox, incoming)))

    def info_copies(ox, oy, oz, incoming):
        mine, theirs = oz * 9 + slot_of(ox, oy), oz * 9 + slot_of(-ox, -oy)
        target = device(ox, oy, oz)
        if incoming:
            return remote(info_send, info_recv.at[oz, slot_of(ox, oy)], info_ss.at[mine], info_rs.at[mine], target)
        return remote(info_send, info_recv.at[oz, slot_of(-ox, -oy)], info_ss.at[mine], info_rs.at[theirs], target)

    def for_info(fn, incoming=False):
        for ox, oy, oz in NEIGHBOURS:
            guarded(exists(ox, oy), lambda ox=ox, oy=oy, oz=oz: fn(info_copies(ox, oy, oz, incoming)))

    def pack_halo(k):
        packed = zero
        for p in range(2):
            for x in range(CX):
                for t in range(TILES):
                    v = cor[k, p, pl.ds((x + 1) * PY + 8 + 8 * t, 8), :]
                    to = p * 32 + t * 8 + x
                    packed = jnp.where(lane == to, pltpu.roll(v, jnp.where(iz == 0, to + 1, to), 1), packed)
        stage[k, 2] = packed
        stage[k, 5] = packed
        for p in range(2):
            stage[k, p] = cor[k, p, pl.ds(PY + 8, 8, stride=PY), :]
            stage[k, 3 + p] = cor[k, p, pl.ds(PY + 39, 8, stride=PY), :]
        lines = [cor[k, p, pl.ds(x * PY + y, 1), :] for p in range(2) for x in (1, 8) for y in (8, 39)]
        stage[k, 6] = jnp.concatenate(lines, axis=0)

    def reduce_copies(k, stage_no, every=True):
        bufs, srcs, targets = ((ar1, ar_src1, group1), (ar2, ar_src2, group2))[stage_no]
        sem = 2 * k + stage_no
        if every:
            return remote(bufs.at[k], bufs.at[k], ar_ss.at[sem], ar_rs.at[sem], targets[0])
        return [remote(srcs.at[k], bufs.at[k, d], ar_ss.at[sem], ar_rs.at[sem], target)
                for d, target in enumerate(targets)]

    def reduce_start(k, stage_no):
        for send in reduce_copies(k, stage_no, False):
            send.start()

    def reduce_finish(k, stage_no):
        bufs, srcs, targets = ((ar1, ar_src1, group1), (ar2, ar_src2, group2))[stage_no]
        reduce_copies(k, stage_no).wait_recv()
        total = srcs[k]
        for d in range(len(targets)):
            total = total + bufs[k, d]
        return total

    def setup_rounds():
        rows = []
        for s in range(2):
            tiles = {o: info_recv[s, slot_of(*o)] for o in OFFSETS}
            if s == 0:
                tiles[(0, 0)] = info_send[...]
            roles = assemble(tiles, -1.0)
            coltile[4 * s + 0] = roles[0]
            coltile[4 * s + 1] = roles[2]
            coltile[4 * s + 2] = roll(roles[0], -32)
            coltile[4 * s + 3] = roll(roles[1], -32)
            if s == 0:
                for role in range(4):
                    coltile[8 + role] = roll(roles[role], -64)
                corner = [jnp.full((4, 128), -1.0, F32) for _ in range(4)]
                row4 = iota(0, (4, 128))
                for j, tile in enumerate((roles[0], roles[2], roll(roles[0], -32), roll(roles[1], -32))):
                    for c in range(4):
                        sx, sy = c // 2, c % 2
                        spot = (lane == (3 * sy) * 8 + 7 * sx) & (sub == 7 * sy)
                        value = jnp.max(jnp.max(jnp.where(spot, tile, -1.0), axis=1, keepdims=True), axis=0, keepdims=True)
                        corner[j] = jnp.where(row4 == c, value, corner[j])
                    edgecol[j] = corner[j]
            ids_row = jnp.full((8, 128), -1.0, F32)
            for role in range(4):
                spread = jnp.broadcast_to(jnp.max(roles[role], axis=0, keepdims=True), (8, 128))
                ids_row = jnp.where(lane // 32 == role, roll(spread, 32 * (role + 1)), ids_row)
            rows.append(ids_row[0:1])
        number = iota(0, (128, 128)).astype(F32)
        for s in range(2):
            wide = jnp.broadcast_to(rows[s], (128, 128))
            for j in range(4):
                onehot[:, pl.ds((4 * s + j) * 128, 128)] = jnp.where(wide - 128.0 * j == number, 1.0, 0.0).astype(BF16)

    def coarse_rows(totals):
        kt = ktile[...]
        swapped = pltpu.roll(totals, 4, 0)
        k_swap = pltpu.roll(kt, 4, 0)
        k_all = jnp.where(low_rows, kt, k_swap)
        d_all = jnp.where(low_rows, k_swap, kt)
        norm = k_all * k_all + d_all * d_all
        norm = jnp.where(norm > 0.0, norm, 1.0)
        c = (jnp.where(low_rows, swapped, -swapped) * d_all - totals * k_all) / norm
        high = c.astype(BF16)
        rest = c - high.astype(F32)
        middle = rest.astype(BF16)
        low = (rest - middle.astype(F32)).astype(BF16)
        split = jnp.concatenate([high.astype(F32), middle.astype(F32), low.astype(F32), zero], axis=0).astype(BF16)
        found = jnp.dot(split, onehot[...], preferred_element_type=F32)
        found = found[0:8] + found[8:16] + found[16:24]
        rows = []
        for s in range(2):
            spread = zero
            for j in range(4):
                spread = spread + jnp.where(sub % 4 == j, found[:, (4 * s + j) * 128:(4 * s + j + 1) * 128], 0.0)
            rows.append([jnp.sum(spread[0:4], axis=0, keepdims=True), jnp.sum(spread[4:8], axis=0, keepdims=True)])
        return rows

    def sides_rounds(k):
        cells = []
        for s in range(2):
            tiles = {}
            for ox, oy in OFFSETS:
                if s == 0 and ox == 0 and oy == 0:
                    tiles[(ox, oy)] = stage[k, 2]
                elif s == 0 and ox and oy:
                    tiles[(ox, oy)] = rd[k, corner_of(ox, oy), 0]
                elif s == 0 and oy:
                    tiles[(ox, oy)] = ry[k, 0, 0] if oy < 0 else ry[k, 1, 2]
                else:
                    tiles[(ox, oy)] = rz[k, s, slot_of(ox, oy)]
            roles = assemble(tiles, 0.0)
            cells.append([(role, roll(role, -32)) for role in roles])
        for r in range(6):
            now = float(r)
            for s in range(2):
                c = cells[s]
                c[0], c[1] = blend(c[0], c[1], coltile[4 * s + 0] == now)
                c[2], c[3] = blend(c[2], c[3], coltile[4 * s + 1] == now)
                c[0], c[2] = blend(c[0], c[2], coltile[4 * s + 2] == now)
                c[1], c[3] = blend(c[1], c[3], coltile[4 * s + 3] == now)
            for role in range(4):
                cells[0][role], cells[1][role] = blend(cells[0][role], cells[1][role], coltile[8 + role] == now)
        return cells

    def main_rounds(k):
        def lines(planes, rows):
            return tuple(
                jnp.concatenate([cor[k, p, pl.ds(x * PY + y, 1), :] for x in planes for y in rows], axis=0) for p in range(2))

        c0 = lines((1, 8), (8, 39))
        px = lines((0, 9), (8, 39))
        halo_rows = []
        for p in range(2):
            parts = []
            for x_at in (0, 7):
                parts += [ry[k, 0, 1 + p, pl.ds(x_at, 1), :], ry[k, 1, p, pl.ds(x_at, 1), :]]
            halo_rows.append(jnp.concatenate(parts, axis=0))
        py = tuple(halo_rows)
        diagonal = []
        for p in range(2):
            parts = []
            for c in range(4):
                parts.append(rd[k, c, 1, pl.ds(p * 4 + (3 - c), 1), :])
            diagonal.append(jnp.concatenate(parts, axis=0))
        pxy = tuple(diagonal)
        for r in range(6):
            now = float(r)
            c0, px = blend(c0, px, edgecol[0] == now)
            py, pxy = blend(py, pxy, edgecol[1] == now)
            c0, py = blend(c0, py, edgecol[2] == now)
            px, pxy = blend(px, pxy, edgecol[3] == now)
        for own, halo, ox in ((1, 0, -1), (8, 9, 1)):
            a = tuple(cor[k, p, pl.ds(own * PY + 8, 32), :] for p in range(2))
            b = tuple(cor[k, p, pl.ds(halo * PY + 8, 32), :] for p in range(2))
            a, b = blend(a, b, jnp.broadcast_to(has_x[ox], (32, 128)))
            for p in range(2):
                cor[k, p, pl.ds(own * PY + 8, 32), :] = a[p]
                cor[k, p, pl.ds(halo * PY + 8, 32), :] = b[p]
        for own, halo, oy in ((8, 7, -1), (39, 40, 1)):
            a = tuple(stage[k, p if oy < 0 else 3 + p] for p in range(2))
            b = tuple(ry[k, 0, 1 + p] if oy < 0 else ry[k, 1, p] for p in range(2))
            a, b = blend(a, b, jnp.broadcast_to(has_y[oy], (8, 128)))
            for p in range(2):
                cor[k, p, pl.ds(PY + own, 8, stride=PY), :] = a[p]
                cor[k, p, pl.ds(PY + halo, 8, stride=PY), :] = b[p]
        for c in range(4):
            sx, sy = c // 2, c % 2
            own_x, halo_x = (1, 8)[sx], (0, 9)[sx]
            own_y, halo_y = (8, 39)[sy], (7, 40)[sy]
            for p in range(2):
                cor[k, p, pl.ds(own_x * PY + own_y, 1), :] = c0[p][c:c + 1]
                cor[k, p, pl.ds(halo_x * PY + own_y, 1), :] = px[p][c:c + 1]
                cor[k, p, pl.ds(own_x * PY + halo_y, 1), :] = py[p][c:c + 1]
                cor[k, p, pl.ds(halo_x * PY + halo_y, 1), :] = pxy[p][c:c + 1]

    def update(k, cells, coarse):
        last = k == SWEEPS - 1
        for p in range(2):
            turned = [pltpu.roll(cells[0][role][p], zf, 1) for role in range(4)]
            row = coarse[0][p]

            def term(role, t, x):
                at = 32 * role + 8 * t + x
                return jnp.broadcast_to(row[:, at:at + 1], (8, 128))

            for x in range(10):
                if last and x in (0, 9):
                    continue
                role = 1 if x in (0, 9) else 0
                near = min(max(x - 1, 0), 7)
                for t in range(TILES):
                    value = term(role, t, (near // 4) * 4 if role == 0 else near)
                    column = roll(turned[role], -(8 * t + near))
                    rows = pl.ds(x * PY + 8 + 8 * t, 8)
                    value = value + fld[p, rows, :] + jnp.where(at_face, column, cor[k, p, rows, :])
                    if last:
                        out[p, x - 1, pl.ds(8 * t, 8), :] = value
                    else:
                        fld[p, rows, :] = value
                if last:
                    continue
                for t, at, y in ((0, 0, 7), (TILES - 1, 7, 40)):
                    column = roll(turned[2 + role], -(8 * t + near))[at:at + 1]
                    place = pl.ds(x * PY + y, 1)
                    value = term(2 + role, t, near)[0:1] + fld[p, place, :]
                    fld[p, place, :] = value + jnp.where(at_face[0:1], column, cor[k, p, place, :])
            if not last:
                for role in range(4):
                    here_row = jnp.broadcast_to(coarse[1][p], (8, 128))
                    fz[role, p] = fz[role, p] + cells[1][role][p] + roll(here_row, -32 * role)

    for k in range(SWEEPS):
        sums = first_pass() if k == 0 else residual_pass()
        ar_src1[k] = bucket(sums)
        if k == 0:
            jacobi(k)
            pack_halo(k)
            pl.semaphore_wait(barrier, count)
            reduce_start(k, 0)
            reduce_start(SWEEPS, 0)
            for_info(lambda copy: copy.start())
            for_halo(k, lambda copy: copy.start())
        else:
            reduce_start(k, 0)
            jacobi(k)
            pack_halo(k)
            for_halo(k, lambda copy: copy.start())
        ar_src2[k] = reduce_finish(k, 0)
        reduce_start(k, 1)
        if k == 0:
            ar_src2[SWEEPS] = reduce_finish(SWEEPS, 0)
            reduce_start(SWEEPS, 1)
            for_info(lambda copy: copy.wait_recv(), True)
            setup_rounds()
        for_halo(k, lambda copy: copy.wait_recv(), True)
        cells = sides_rounds(k)
        for_halo(k, lambda copy: copy.wait_send())
        main_rounds(k)
        reduce_copies(k, 0).wait_send()
        if k == 0:
            reduce_copies(SWEEPS, 0).wait_send()
            for_info(lambda copy: copy.wait_send())
            ktile[...] = reduce_finish(SWEEPS, 1)
            reduce_copies(SWEEPS, 1).wait_send()
        coarse = coarse_rows(reduce_finish(k, 1))
        update(k, cells, coarse)
        reduce_copies(k, 1).wait_send()


def solution(mesh):
    nx, ny = mesh.shape["gx"], mesh.shape["gy"]

    def step(adjoint_source, velocity, damping, face_rounds, aggregates):
        vmem = pl.BlockSpec(memory_space=pltpu.VMEM)
        smem = pl.BlockSpec(memory_space=pltpu.SMEM)
        dma = pltpu.SemaphoreType.DMA
        tile = (8, 128)
        block = (CX, CY, CZ)
        return pl.pallas_call(
            functools.partial(kernel, nx, ny),
            out_shape=jax.ShapeDtypeStruct((2,) + block, F32),
            in_specs=[vmem, vmem, vmem, smem, smem],
            out_specs=vmem,
            scratch_shapes=[
                pltpu.VMEM(block, F32), pltpu.VMEM(block, F32), pltpu.VMEM(block, F32), pltpu.VMEM(block, F32),
                pltpu.VMEM((2,) + block, F32),
                pltpu.VMEM((2, CX * PY, CZ), F32), pltpu.VMEM((2, CX * PY, CZ), F32),
                pltpu.VMEM((SWEEPS, 2, 10 * PY, CZ), F32),
                pltpu.VMEM((2, 10 * PY, CZ), F32),
                pltpu.VMEM((4, 2) + tile, F32),
                pltpu.VMEM((12,) + tile, F32), pltpu.VMEM((4, 4, 128), F32),
                pltpu.VMEM((128, 1024), BF16), pltpu.VMEM(tile, F32),
                pltpu.VMEM(tile, F32), pltpu.VMEM((2, 9) + tile, F32),
                pltpu.VMEM((SWEEPS, 7) + tile, F32), pltpu.VMEM((SWEEPS, 2, 9) + tile, F32),
                pltpu.VMEM((SWEEPS, 2, 3) + tile, F32), pltpu.VMEM((SWEEPS, 4, 2) + tile, F32),
                pltpu.VMEM((SWEEPS + 1,) + tile, F32), pltpu.VMEM((SWEEPS + 1,) + tile, F32),
                pltpu.VMEM((SWEEPS + 1, nx - 1) + tile, F32), pltpu.VMEM((SWEEPS + 1, 2 * ny - 1) + tile, F32),
                dma((18,)), dma((18,)), dma((SWEEPS, 18)), dma((SWEEPS, 18)),
                dma((SWEEPS, 2)), dma((SWEEPS, 2)), dma((2 * SWEEPS + 2,)), dma((2 * SWEEPS + 2,)),
            ],
            compiler_params=pltpu.CompilerParams(
                collective_id=0, has_side_effects=True, vmem_limit_bytes=32 * 1024 * 1024
            ),
        )(adjoint_source, velocity, damping, face_rounds, aggregates)

    placed = (
        P(None, "gx", "gy", "gz"),
        P("gx", "gy", "gz"),
        P("gx", "gy", "gz"),
        P("gx", "gy", "gz", None),
        P("gx", "gy", "gz"),
    )
    return jax.shard_map(
        step, mesh=mesh, in_specs=placed, out_specs=P(None, "gx", "gy", "gz"), check_vma=False
    )
```

profile of v0, /device:TPU:1, one launch (start us, length us, event | category | flops | bytes accessed | tf_op | source)
XLA Modules:
  0.0 49.5 jit_solution(11936990907121394545)
XLA Ops:
  0.0 0.0 copy-start.3
  0.0 0.8 %copy.6.aggs = s32[2,4,1]{2,1,0:T(4,128)S(1)} copy(s32[2,4,1]{1,2,0:T(1,128)} %param.9) | data formatting | bytes 64 | tf_op args[4]
  0.8 0.0 copy-done.3
  0.8 0.0 copy-start
  0.8 0.9 %copy-done = f32[2,8,32,128]{3,2,1,0:T(8,128)S(1)} copy-done((f32[2,8,32,128]{3,2,1,0:T(8,128)S(1)}, f32[2,8,32,128]{3,2,1,0:T(8,128)}, u32[]{:S(2)}) %copy-start) | copy-done | bytes 262168
  1.7 0.0 copy-start.1
  1.7 0.9 %copy-done.1 = f32[8,32,128]{2,1,0:T(8,128)S(1)} copy-done((f32[8,32,128]{2,1,0:T(8,128)S(1)}, f32[8,32,128]{2,1,0:T(8,128)}, u32[]{:S(2)}) %copy-start.1) | copy-done | bytes 131096
  2.6 0.0 copy-start.2
  2.6 0.9 %copy-done.2 = f32[8,32,128]{2,1,0:T(8,128)S(1)} copy-done((f32[8,32,128]{2,1,0:T(8,128)S(1)}, f32[8,32,128]{2,1,0:T(8,128)}, u32[]{:S(2)}) %copy-start.2) | copy-done | bytes 131096
  3.5 45.2 %shard_map.55 = f32[2,8,32,128]{3,2,1,0:T(8,128)S(1)} custom-call(f32[2,8,32,128]{3,2,1,0:T(8,128)S(1)} %copy-done, f32[8,32,128]{2,1,0:T(8,128)S(1)} %copy-done.1, f32[8,32,128]{2,1,0:T(8,128)S(1)} %copy-done.2, s32[1,1,1,6]{3,2,1,0:T(1,128)S(1)} %copy-done.3, s32[2,4,1]{2,1,0:T(4,128)S(1)} %copy.6.aggs), custom_call_target="tpu_custom_call" | custom-call | tf_op jit(solution)/shard_map/pallas_call | solution.py:627
  48.8 0.7 %copy.8 = f32[2,8,32,128]{3,2,1,0:T(8,128)} copy(f32[2,8,32,128]{3,2,1,0:T(8,128)S(1)} %shard_map.55) | data formatting | bytes 524288
Async XLA Ops:
  0.0 0.8 %copy-start.3 = (s32[1,1,1,6]{3,2,1,0:T(1,128)S(1)}, s32[1,1,1,6]{3,2,1,0:T(1,128)}, u32[]{:S(2)}) copy-start(s32[1,1,1,6]{3,2,1,0:T(1,128)} %rounds.1) | copy-start | bytes 76
  0.8 1.0 %copy-start = (f32[2,8,32,128]{3,2,1,0:T(8,128)S(1)}, f32[2,8,32,128]{3,2,1,0:T(8,128)}, u32[]{:S(2)}) copy-start(f32[2,8,32,128]{3,2,1,0:T(8,128)} %src.1) | copy-start | bytes 786436
  1.7 0.9 %copy-start.1 = (f32[8,32,128]{2,1,0:T(8,128)S(1)}, f32[8,32,128]{2,1,0:T(8,128)}, u32[]{:S(2)}) copy-start(f32[8,32,128]{2,1,0:T(8,128)} %vel.1) | copy-start | bytes 393220
  2.6 0.9 %copy-start.2 = (f32[8,32,128]{2,1,0:T(8,128)S(1)}, f32[8,32,128]{2,1,0:T(8,128)}, u32[]{:S(2)}) copy-start(f32[8,32,128]{2,1,0:T(8,128)} %dmp.1) | copy-start | bytes 393220
where the time goes:
time: 49.6 us; the launch traced here: 49.5 us
  Pallas kernels  45.2 us (91%)
  local copies, waits for them, and re-layouts  4.25 us (9%)
    pallas_call x1, Pallas kernels, step(): pl.pallas_call(functools.partial(kernel, nx, ny), out_shape=jax.ShapeDtyp...  45.2 us
    unnamed x10, local copies, waits for them, and re-layouts  4.25 us

commit v1 on v0

--- a/solution.py
+++ b/solution.py
@@ -64,11 +64,12 @@
 
 def kernel(
     nx, ny,
-    src, vel, dmp, rounds, aggs, out,
+    src_in, vel_in, dmp_in, rounds, aggs, out,
+    src, vel, dmp, in_sem,
     kap, kdm, mre, mim, res, ping, pong, cor, fld, fz,
-    coltile, edgecol, onehot, ktile,
-    info_send, info_recv, stage, rz, ry, rd, ar_src1, ar_src2, ar1, ar2,
-    info_ss, info_rs, h_ss, h_rs, x_ss, x_rs, ar_ss, ar_rs,
+    coltile, edgecol, onehot, ksum, cval, zmask,
+    info_send, info_recv, stage, rz, ry, rd, row_send, pair_recv, chip_send, gath,
+    info_ss, info_rs, h_ss, h_rs, x_ss, x_rs, pair_ss, pair_rs, ga_ss, ga_rs,
 ):
     ix, iy, iz = lax.axis_index("gx"), lax.axis_index("gy"), lax.axis_index("gz")
     lane, sub = iota(1), iota(0)
@@ -100,12 +101,29 @@
     def device(ox, oy, oz):
         return (ix + ox, iy + oy, (1 - iz) if oz else iz)
 
-    group1 = [(lax.rem(ix + d, nx), iy, iz) for d in range(1, nx)]
-    here = iz * ny + iy
-    group2 = []
-    for d in range(1, 2 * ny):
-        there = lax.rem(here + d, 2 * ny)
-        group2.append((ix, lax.rem(there, ny), there // ny))
+    core = lax.rem(iy, 2)
+    at_x, at_y, at_z = lax.rem(ix, 4), ix // 4, iz * (ny // 2) + iy // 2
+    nz = ny
+    pair = (ix, iy + 1 - 2 * core, iz)
+    across = sorted(((dx, dy) for dx in range(4) for dy in range(4)), key=lambda d: -min(d[0], 4 - d[0]) - min(d[1], 4 - d[1]))
+    across_x = [lax.rem(at_y + dy, 4) * 4 + lax.rem(at_x + dx, 4) for dx, dy in across]
+
+    def for_chips(fn):
+        def layer(i, carry):
+            step = (i + 1) // 2
+            there = lax.rem(at_z + nz // 2 + jnp.where(lax.rem(i, 2) == 1, nz - step, step), nz)
+            ty, tz = lax.rem(there, ny // 2) * 2 + core, there // (ny // 2)
+            for j in range(16):
+                fn(i * 16 + j, (across_x[j], ty, tz))
+            return carry
+        lax.fori_loop(0, nz - 1, layer, 0)
+        for j in range(15):
+            fn((nz - 1) * 16 + j, (across_x[j], iy, iz))
+
+    loads = [pltpu.make_async_copy(whole, local, in_sem.at[i])
+             for i, (whole, local) in enumerate(((vel_in, vel), (dmp_in, dmp), (src_in, src)))]
+    for load in loads:
+        load.start()
 
     zero = jnp.zeros((8, 128), F32)
     for k in range(SWEEPS):
@@ -128,15 +146,20 @@
             info_recv[s, o] = zero - 1.0
 
     barrier = pltpu.get_barrier_semaphore()
-    count = jnp.int32(nx - 1 + 2 * ny - 1 + 1)
+    count = jnp.int32(16 * nz - 1 + 1)
     for ox, oy, oz in NEIGHBOURS:
+        if oy == 0:
+            continue
         def tell(ox=ox, oy=oy, oz=oz):
             pl.semaphore_signal(barrier, inc=1, device_id=device(ox, oy, oz), device_id_type=MESH)
         guarded(exists(ox, oy), tell)
-        if exists(ox, oy) is not None:
-            count = count + jnp.where(exists(ox, oy), 1, 0)
-    for target in group2 + group1:
+        count = count + jnp.where(exists(ox, oy), 1, 0)
+
+    def tell_chip(slot, target):
         pl.semaphore_signal(barrier, inc=1, device_id=target, device_id_type=MESH)
+
+    for_chips(tell_chip)
+    tell_chip(0, pair)
 
     for buf in (ping, pong):
         for p in range(2):
@@ -150,6 +173,8 @@
         for role in range(4):
             fz[role, p] = zero
 
+    for load in loads:
+        load.wait()
     for x in range(CX):
         v = vel[x]
         kappa = OMEGA_SQ / (v * v)
@@ -167,7 +192,7 @@
     low_x, high_x = face(0, ix > 0), face(1, ix < nx - 1)
     low_y, high_y = face(2, iy > 0), face(3, iy < ny - 1)
     depth = jnp.where(iz == 0, rounds[0, 0, 0, 5].astype(F32), rounds[0, 0, 0, 4].astype(F32))
-    ids = [[aggs[qx, qy, 0].astype(F32) for qy in range(TILES)] for qx in range(2)]
+    ids = [[aggs[qx, 0, qy].astype(F32) for qy in range(TILES)] for qx in range(2)]
     info = jnp.where(lx == 0, low_x, jnp.where(lx == 7, high_x, -1.0))
     col_y = jnp.where((lt == 0) & (sub == 0), low_y, jnp.where((lt == TILES - 1) & (sub == 7), high_y, -1.0))
     info = jnp.where(lane >= 32, col_y, info)
@@ -177,20 +202,14 @@
             info = jnp.where((lane >= 96) & (lx // 4 == qx) & (lt == qy), ids[qx][qy], info)
     info_send[...] = info
 
-    agg_of = ((sub % 4) * 128 + lane).astype(F32)
     low_rows = sub < 4
-
-    def bucket(sums):
+    lane1 = iota(1, (1, 128))
+
+    def row_of(sums, first):
         rows = [jnp.sum(sums[p][qx][t], axis=0, keepdims=True) for p in range(2) for qx in range(2) for t in range(TILES)]
         total = jnp.sum(jnp.concatenate(rows, axis=0), axis=1, keepdims=True)
-        tile = zero
-        for qx in range(2):
-            for t in range(TILES):
-                q = qx * TILES + t
-                s_re = jnp.broadcast_to(total[q:q + 1], (8, 128))
-                s_im = jnp.broadcast_to(total[8 + q:9 + q], (8, 128))
-                tile = jnp.where(agg_of == ids[qx][t], tile + jnp.where(low_rows, s_re, s_im), tile)
-        return tile
+        spread = jnp.where(iota(1, (16, 128)) == iota(0, (16, 128)) + first, jnp.broadcast_to(total, (16, 128)), 0.0)
+        return jnp.sum(spread, axis=0, keepdims=True)
 
     def rows_of(v, t):
         return v[8 * t:8 * t + 8]
@@ -201,7 +220,10 @@
         for t in range(TILES):
             sums[0][x // 4][t] = sums[0][x // 4][t] + rows_of(kappa, t)
             sums[1][x // 4][t] = sums[1][x // 4][t] + rows_of(damp, t)
-    ar_src1[SWEEPS] = bucket(sums)
+    fixed_row = row_of(sums, 32 + 16 * core)
+    for qx in range(2):
+        for t in range(TILES):
+            fixed_row = fixed_row + jnp.where(lane1 == 64 + 8 * core + qx * TILES + t, ids[qx][t], 0.0)
 
     def assemble(tiles, default):
         def pick(parts):
@@ -385,28 +407,48 @@
         lines = [cor[k, p, pl.ds(x * PY + y, 1), :] for p in range(2) for x in (1, 8) for y in (8, 39)]
         stage[k, 6] = jnp.concatenate(lines, axis=0)
 
-    def reduce_copies(k, stage_no, every=True):
-        bufs, srcs, targets = ((ar1, ar_src1, group1), (ar2, ar_src2, group2))[stage_no]
-        sem = 2 * k + stage_no
-        if every:
-            return remote(bufs.at[k], bufs.at[k], ar_ss.at[sem], ar_rs.at[sem], targets[0])
-        return [remote(srcs.at[k], bufs.at[k, d], ar_ss.at[sem], ar_rs.at[sem], target)
-                for d, target in enumerate(targets)]
-
-    def reduce_start(k, stage_no):
-        for send in reduce_copies(k, stage_no, False):
-            send.start()
-
-    def reduce_finish(k, stage_no):
-        bufs, srcs, targets = ((ar1, ar_src1, group1), (ar2, ar_src2, group2))[stage_no]
-        reduce_copies(k, stage_no).wait_recv()
-        total = srcs[k]
-        for d in range(len(targets)):
-            total = total + bufs[k, d]
-        return total
+    first_row = pl.ds(0, 1)
+    others = pl.ds(0, 16 * nz - 1)
+
+    def pair_copy(k):
+        return remote(row_send.at[k, first_row], pair_recv.at[k, first_row], pair_ss.at[k], pair_rs.at[k], pair)
+
+    def gather_start(k):
+        chip = row_send[k, first_row] + pair_recv[k, first_row]
+        chip_send[k, first_row] = chip
+        gath[k, pl.ds(16 * nz - 1, 1)] = chip
+        for_chips(lambda slot, target: remote(
+            chip_send.at[k, first_row], gath.at[k, pl.ds(slot, 1)], ga_ss.at[k], ga_rs.at[k], target).start())
+
+    def gather_every(k):
+        return remote(gath.at[k, others], gath.at[k, others], ga_ss.at[k], ga_rs.at[k], pair)
+
+    lane_n = iota(1, (128, 128))
+
+    def by_aggregate(values):
+        whole = jnp.where(lane_n < 32, values, 0.0)
+        high = whole.astype(BF16).astype(F32)
+        rest = whole - high
+        middle = rest.astype(BF16).astype(F32)
+        split = high + pltpu.roll(middle, 32, 1) + pltpu.roll(rest - middle, 64, 1)
+        found = jnp.dot(onehot[...], split.astype(BF16), preferred_element_type=F32)
+        lane64 = iota(1, (64, 128))
+        total = jnp.zeros((64, 128), F32)
+        for b in range(16):
+            mine = (lane64 % 8 == b % 8) & ((lane64 // 16) % 2 == b // 8)
+            total = jnp.where(mine, found[64 * b:64 * b + 64], total)
+        total = jnp.where(lane64 < 96, total, 0.0)
+        real = (lane64 // 8) % 2 == 0
+        return (jnp.sum(jnp.where(real, total, 0.0), axis=1, keepdims=True),
+                jnp.sum(jnp.where(real, 0.0, total), axis=1, keepdims=True))
+
+    row64 = iota(0, (64, 128))
+
+    def place_of(row):
+        return row // 24, (row % 24) // 6, row % 6
 
     def setup_rounds():
-        rows = []
+        found = jnp.full((64, 128), -1.0, F32)
         for s in range(2):
             tiles = {o: info_recv[s, slot_of(*o)] for o in OFFSETS}
             if s == 0:
@@ -428,40 +470,46 @@
                         value = jnp.max(jnp.max(jnp.where(spot, tile, -1.0), axis=1, keepdims=True), axis=0, keepdims=True)
                         corner[j] = jnp.where(row4 == c, value, corner[j])
                     edgecol[j] = corner[j]
-            ids_row = jnp.full((8, 128), -1.0, F32)
+            lane64 = iota(1, (64, 128))
+            side, at_qx, at_qy = place_of(row64)
+            role_at = jnp.where((at_qx == 0) | (at_qx == 3), 1, 0) + jnp.where((at_qy == 0) | (at_qy == 5), 2, 0)
+            x_at = jnp.where(at_qx == 2, 4, jnp.where(at_qx == 3, 7, 0))
+            spot = 96 + 8 * jnp.clip(at_qy - 1, 0, TILES - 1) + x_at
             for role in range(4):
-                spread = jnp.broadcast_to(jnp.max(roles[role], axis=0, keepdims=True), (8, 128))
-                ids_row = jnp.where(lane // 32 == role, roll(spread, 32 * (role + 1)), ids_row)
-            rows.append(ids_row[0:1])
-        number = iota(0, (128, 128)).astype(F32)
-        for s in range(2):
-            wide = jnp.broadcast_to(rows[s], (128, 128))
-            for j in range(4):
-                onehot[:, pl.ds((4 * s + j) * 128, 128)] = jnp.where(wide - 128.0 * j == number, 1.0, 0.0).astype(BF16)
-
-    def coarse_rows(totals):
-        kt = ktile[...]
-        swapped = pltpu.roll(totals, 4, 0)
-        k_swap = pltpu.roll(kt, 4, 0)
-        k_all = jnp.where(low_rows, kt, k_swap)
-        d_all = jnp.where(low_rows, k_swap, kt)
-        norm = k_all * k_all + d_all * d_all
+                spread = jnp.broadcast_to(jnp.max(roles[role], axis=0, keepdims=True), (64, 128))
+                found = jnp.where((side == s) & (role_at == role) & (lane64 == spot), spread, found)
+        wanted = jnp.broadcast_to(jnp.max(found, axis=1, keepdims=True), (64, 128))
+        cval[0] = wanted
+        row24 = iota(0, (24, 128))
+        lane24 = iota(1, (24, 128))
+        x24, t24 = lane24 % 8, (lane24 // 8) % TILES
+        for role in range(4):
+            if role % 2:
+                want_x = jnp.where(x24 == 0, 0, jnp.where(x24 == 7, 3, -1))
+            else:
+                want_x = 1 + x24 // 4
+            if role // 2:
+                want_y = jnp.where(t24 == 0, 0, jnp.where(t24 == TILES - 1, 5, -1))
+            else:
+                want_y = 1 + t24
+            zmask[role] = jnp.where((row24 // 6 == want_x) & (row24 % 6 == want_y), 1.0, 0.0)
+
+    def setup_aggregates():
+        wanted = cval[0]
+        cells = jnp.transpose(gath[0])
+        for b in range(16):
+            row = jnp.broadcast_to(cells[64 + b:65 + b], (64, 128))
+            onehot[pl.ds(64 * b, 64), :] = jnp.where(wanted == row, 1.0, 0.0).astype(BF16)
+        for p, total in enumerate(by_aggregate(pltpu.roll(gath[0], 96, 1))):
+            ksum[p] = jnp.broadcast_to(total, (64, 128))
+
+    def coarse_values(k):
+        r_re, r_im = by_aggregate(gath[k])
+        k_re, k_im = ksum[0], ksum[1]
+        norm = k_re * k_re + k_im * k_im
         norm = jnp.where(norm > 0.0, norm, 1.0)
-        c = (jnp.where(low_rows, swapped, -swapped) * d_all - totals * k_all) / norm
-        high = c.astype(BF16)
-        rest = c - high.astype(F32)
-        middle = rest.astype(BF16)
-        low = (rest - middle.astype(F32)).astype(BF16)
-        split = jnp.concatenate([high.astype(F32), middle.astype(F32), low.astype(F32), zero], axis=0).astype(BF16)
-        found = jnp.dot(split, onehot[...], preferred_element_type=F32)
-        found = found[0:8] + found[8:16] + found[16:24]
-        rows = []
-        for s in range(2):
-            spread = zero
-            for j in range(4):
-                spread = spread + jnp.where(sub % 4 == j, found[:, (4 * s + j) * 128:(4 * s + j + 1) * 128], 0.0)
-            rows.append([jnp.sum(spread[0:4], axis=0, keepdims=True), jnp.sum(spread[4:8], axis=0, keepdims=True)])
-        return rows
+        cval[0] = (r_im * k_im - r_re * k_re) / norm
+        cval[1] = (-r_re * k_im - r_im * k_re) / norm
 
     def sides_rounds(k):
         cells = []
@@ -541,15 +589,15 @@
                 cor[k, p, pl.ds(own_x * PY + halo_y, 1), :] = py[p][c:c + 1]
                 cor[k, p, pl.ds(halo_x * PY + halo_y, 1), :] = pxy[p][c:c + 1]
 
-    def update(k, cells, coarse):
+    def update(k, cells):
         last = k == SWEEPS - 1
         for p in range(2):
             turned = [pltpu.roll(cells[0][role][p], zf, 1) for role in range(4)]
-            row = coarse[0][p]
 
             def term(role, t, x):
-                at = 32 * role + 8 * t + x
-                return jnp.broadcast_to(row[:, at:at + 1], (8, 128))
+                at_qx = (0 if x == 0 else 3) if role % 2 else 1 + x // 4
+                at_qy = (0 if t == 0 else 5) if role // 2 else 1 + t
+                return jnp.broadcast_to(cval[p, pl.ds(at_qx * 6 + at_qy, 1), :], (8, 128))
 
             for x in range(10):
                 if last and x in (0, 9):
@@ -573,46 +621,43 @@
                     value = term(2 + role, t, near)[0:1] + fld[p, place, :]
                     fld[p, place, :] = value + jnp.where(at_face[0:1], column, cor[k, p, place, :])
             if not last:
+                other = cval[p, pl.ds(24, 24), :]
                 for role in range(4):
-                    here_row = jnp.broadcast_to(coarse[1][p], (8, 128))
-                    fz[role, p] = fz[role, p] + cells[1][role][p] + roll(here_row, -32 * role)
+                    halo = jnp.broadcast_to(jnp.sum(other * zmask[role], axis=0, keepdims=True), (8, 128))
+                    fz[role, p] = fz[role, p] + cells[1][role][p] + halo
 
     for k in range(SWEEPS):
-        sums = first_pass() if k == 0 else residual_pass()
-        ar_src1[k] = bucket(sums)
+        row = row_of(first_pass() if k == 0 else residual_pass(), 16 * core)
+        row_send[k, first_row] = row + fixed_row if k == 0 else row
         if k == 0:
             jacobi(k)
             pack_halo(k)
             pl.semaphore_wait(barrier, count)
-            reduce_start(k, 0)
-            reduce_start(SWEEPS, 0)
+            pair_copy(k).start()
             for_info(lambda copy: copy.start())
-            for_halo(k, lambda copy: copy.start())
         else:
-            reduce_start(k, 0)
+            pair_copy(k).start()
             jacobi(k)
             pack_halo(k)
-            for_halo(k, lambda copy: copy.start())
-        ar_src2[k] = reduce_finish(k, 0)
-        reduce_start(k, 1)
+        for_halo(k, lambda copy: copy.start())
+        pair_copy(k).wait_recv()
+        gather_start(k)
         if k == 0:
-            ar_src2[SWEEPS] = reduce_finish(SWEEPS, 0)
-            reduce_start(SWEEPS, 1)
             for_info(lambda copy: copy.wait_recv(), True)
             setup_rounds()
+        pair_copy(k).wait_send()
         for_halo(k, lambda copy: copy.wait_recv(), True)
         cells = sides_rounds(k)
         for_halo(k, lambda copy: copy.wait_send())
         main_rounds(k)
-        reduce_copies(k, 0).wait_send()
         if k == 0:
-            reduce_copies(SWEEPS, 0).wait_send()
             for_info(lambda copy: copy.wait_send())
-            ktile[...] = reduce_finish(SWEEPS, 1)
-            reduce_copies(SWEEPS, 1).wait_send()
-        coarse = coarse_rows(reduce_finish(k, 1))
-        update(k, cells, coarse)
-        reduce_copies(k, 1).wait_send()
+        gather_every(k).wait_recv()
+        if k == 0:
+            setup_aggregates()
+        coarse_values(k)
+        update(k, cells)
+        gather_every(k).wait_send()
 
 
 def solution(mesh):
@@ -620,6 +665,7 @@
 
     def step(adjoint_source, velocity, damping, face_rounds, aggregates):
         vmem = pl.BlockSpec(memory_space=pltpu.VMEM)
+        hbm = pl.BlockSpec(memory_space=pltpu.MemorySpace.HBM)
         smem = pl.BlockSpec(memory_space=pltpu.SMEM)
         dma = pltpu.SemaphoreType.DMA
         tile = (8, 128)
@@ -627,9 +673,10 @@
         return pl.pallas_call(
             functools.partial(kernel, nx, ny),
             out_shape=jax.ShapeDtypeStruct((2,) + block, F32),
-            in_specs=[vmem, vmem, vmem, smem, smem],
+            in_specs=[hbm, hbm, hbm, smem, smem],
             out_specs=vmem,
             scratch_shapes=[
+                pltpu.VMEM((2,) + block, F32), pltpu.VMEM(block, F32), pltpu.VMEM(block, F32), dma((3,)),
                 pltpu.VMEM(block, F32), pltpu.VMEM(block, F32), pltpu.VMEM(block, F32), pltpu.VMEM(block, F32),
                 pltpu.VMEM((2,) + block, F32),
                 pltpu.VMEM((2, CX * PY, CZ), F32), pltpu.VMEM((2, CX * PY, CZ), F32),
@@ -637,19 +684,20 @@
                 pltpu.VMEM((2, 10 * PY, CZ), F32),
                 pltpu.VMEM((4, 2) + tile, F32),
                 pltpu.VMEM((12,) + tile, F32), pltpu.VMEM((4, 4, 128), F32),
-                pltpu.VMEM((128, 1024), BF16), pltpu.VMEM(tile, F32),
+                pltpu.VMEM((1024, 128), BF16), pltpu.VMEM((2, 64, 128), F32), pltpu.VMEM((2, 64, 128), F32),
+                pltpu.VMEM((4, 24, 128), F32),
                 pltpu.VMEM(tile, F32), pltpu.VMEM((2, 9) + tile, F32),
                 pltpu.VMEM((SWEEPS, 7) + tile, F32), pltpu.VMEM((SWEEPS, 2, 9) + tile, F32),
                 pltpu.VMEM((SWEEPS, 2, 3) + tile, F32), pltpu.VMEM((SWEEPS, 4, 2) + tile, F32),
-                pltpu.VMEM((SWEEPS + 1,) + tile, F32), pltpu.VMEM((SWEEPS + 1,) + tile, F32),
-                pltpu.VMEM((SWEEPS + 1, nx - 1) + tile, F32), pltpu.VMEM((SWEEPS + 1, 2 * ny - 1) + tile, F32),
+                pltpu.VMEM((SWEEPS,) + tile, F32), pltpu.VMEM((SWEEPS,) + tile, F32), pltpu.VMEM((SWEEPS,) + tile, F32),
+                pltpu.VMEM((SWEEPS, 128, 128), F32),
                 dma((18,)), dma((18,)), dma((SWEEPS, 18)), dma((SWEEPS, 18)),
-                dma((SWEEPS, 2)), dma((SWEEPS, 2)), dma((2 * SWEEPS + 2,)), dma((2 * SWEEPS + 2,)),
+                dma((SWEEPS, 2)), dma((SWEEPS, 2)), dma((SWEEPS,)), dma((SWEEPS,)), dma((SWEEPS,)), dma((SWEEPS,)),
             ],
             compiler_params=pltpu.CompilerParams(
-                collective_id=0, has_side_effects=True, vmem_limit_bytes=32 * 1024 * 1024
+                collective_id=0, has_side_effects=True, vmem_limit_bytes=64 * 1024 * 1024
             ),
-        )(adjoint_source, velocity, damping, face_rounds, aggregates)
+        )(adjoint_source, velocity, damping, face_rounds, jnp.transpose(aggregates, (0, 2, 1)))
 
     placed = (
         P(None, "gx", "gy", "gz"),

time: 49.6 us -> 45.2 us (0.911)
  local copies, waits for them, and re-layouts: 4.25 us -> 1.67 us
  Pallas kernels: 45.2 us -> 43.3 us
    unnamed x10 -> x1, local copies, waits for them, and re-layouts: 4.25 us -> 1.67 us
    pallas_call x1, Pallas kernels: 45.2 us -> 43.3 us  [step(): pl.pallas_call(functools.partial(kernel, nx, ny), out_shape=jax.ShapeDtyp...]
where the time goes in v1:
time: 45.2 us; the launch traced here: 44.9 us
  Pallas kernels  43.3 us (96%)
  local copies, waits for them, and re-layouts  1.67 us (4%)
    pallas_call x1, Pallas kernels, step(): pl.pallas_call(functools.partial(kernel, nx, ny), out_shape=jax.ShapeDtyp...  43.3 us
    unnamed x1, local copies, waits for them, and re-layouts  1.67 us

profile of v1, /device:TPU:1, one launch (start us, length us, event | category | flops | bytes accessed | tf_op | source)
XLA Modules:
  0.0 44.9 jit_solution(2220174307125114337)
XLA Ops:
  0.0 43.3 %shard_map.55 = f32[2,8,32,128]{3,2,1,0:T(8,128)} custom-call(f32[2,8,32,128]{3,2,1,0:T(8,128)} %src_in.1, f32[8,32,128]{2,1,0:T(8,128)} %vel_in.1, f32[8,32,128]{2,1,0:T(8,128)} %dmp_in.1, s32[1,1,1,6]{3,2,1,0:T(1,128)} %rounds.1, s32[2,1,4]{2,1,0:T(1,128)} %bitcast.3), custom_call_target="tpu_custom_call" | custom-call | tf_op jit(solution)/shard_map/pallas_call | solution.py:673
  43.3 1.7 %copy.8 = f32[2,8,32,128]{3,2,1,0:T(8,128)} copy(f32[2,8,32,128]{3,2,1,0:T(8,128)} %shard_map.55) | data formatting | bytes 524288

commit v2 on v1

--- a/solution.py
+++ b/solution.py
@@ -22,11 +22,7 @@
 OMEGA_SQ = 9.0
 
 OFFSETS = [(ox, oy) for ox in (-1, 0, 1) for oy in (-1, 0, 1)]
-NEIGHBOURS = [(ox, oy, 1) for ox, oy in OFFSETS if ox and oy]
-NEIGHBOURS += [(ox, oy, 1) for ox, oy in OFFSETS if not (ox and oy)]
-NEIGHBOURS += [(ox, oy, 0) for ox, oy in OFFSETS if ox and not oy]
-NEIGHBOURS += [(ox, oy, 0) for ox, oy in OFFSETS if ox and oy]
-NEIGHBOURS += [(ox, oy, 0) for ox, oy in OFFSETS if oy and not ox]
+OFFSETS.sort(key=lambda o: -abs(o[0]) - abs(o[1]))
 
 
 def slot_of(ox, oy):
@@ -68,7 +64,7 @@
     src, vel, dmp, in_sem,
     kap, kdm, mre, mim, res, ping, pong, cor, fld, fz,
     coltile, edgecol, onehot, ksum, cval, zmask,
-    info_send, info_recv, stage, rz, ry, rd, row_send, pair_recv, chip_send, gath,
+    info_send, info_recv, stage, corners, rz, ry, rd, row_send, pair_recv, chip_send, gath,
     info_ss, info_rs, h_ss, h_rs, x_ss, x_rs, pair_ss, pair_rs, ga_ss, ga_rs,
 ):
     ix, iy, iz = lax.axis_index("gx"), lax.axis_index("gy"), lax.axis_index("gz")
@@ -139,21 +135,20 @@
             for j in range(3):
                 ry[k, o, j] = zero
         for o in range(4):
-            for j in range(2):
-                rd[k, o, j] = zero
+            rd[k, o] = zero
     for s in range(2):
         for o in range(9):
             info_recv[s, o] = zero - 1.0
 
     barrier = pltpu.get_barrier_semaphore()
     count = jnp.int32(16 * nz - 1 + 1)
-    for ox, oy, oz in NEIGHBOURS:
-        if oy == 0:
-            continue
-        def tell(ox=ox, oy=oy, oz=oz):
-            pl.semaphore_signal(barrier, inc=1, device_id=device(ox, oy, oz), device_id_type=MESH)
-        guarded(exists(ox, oy), tell)
-        count = count + jnp.where(exists(ox, oy), 1, 0)
+    for ox, oy in OFFSETS:
+        if oy:
+            def tell(ox=ox, oy=oy):
+                for oz in (1, 0):
+                    pl.semaphore_signal(barrier, inc=1, device_id=device(ox, oy, oz), device_id_type=MESH)
+            guarded(exists(ox, oy), tell)
+            count = count + jnp.where(exists(ox, oy), 2, 0)
 
     def tell_chip(slot, target):
         pl.semaphore_signal(barrier, inc=1, device_id=target, device_id_type=MESH)
@@ -352,11 +347,15 @@
         mine, theirs = oz * 9 + slot_of(ox, oy), oz * 9 + slot_of(-ox, -oy)
         target = device(ox, oy, oz)
         if oz == 0 and ox and oy:
-            part = stage.at[k, pl.ds(5, 2)]
-            there, at_home = rd.at[k, corner_of(-ox, -oy)], rd.at[k, corner_of(ox, oy)]
+            part = corners.at[k, corner_of(ox, oy), pl.ds(0, 3)]
+            there, at_home = rd.at[k, corner_of(-ox, -oy), pl.ds(0, 3)], rd.at[k, corner_of(ox, oy), pl.ds(0, 3)]
         elif oz == 0 and oy:
             part = stage.at[k, pl.ds(0, 3)] if oy < 0 else stage.at[k, pl.ds(2, 3)]
             there, at_home = ry.at[k, 1 if oy < 0 else 0], ry.at[k, 0 if oy < 0 else 1]
+        elif oy:
+            leaving, coming = (pl.ds(0, 1), pl.ds(7, 1)) if oy < 0 else (pl.ds(7, 1), pl.ds(0, 1))
+            part = stage.at[k, 2, leaving]
+            there, at_home = rz.at[k, 1, slot_of(-ox, -oy), leaving], rz.at[k, 1, slot_of(ox, oy), coming]
         else:
             part = stage.at[k, 2]
             there, at_home = rz.at[k, oz, slot_of(-ox, -oy)], rz.at[k, oz, slot_of(ox, oy)]
@@ -374,22 +373,52 @@
             return remote(part, at_home, x_ss.at[k, mine], x_rs.at[k, mine], device(ox, 0, 0))
         return remote(part, there, x_ss.at[k, mine], x_rs.at[k, theirs], device(ox, 0, 0))
 
-    def for_halo(k, fn, incoming=False):
-        for ox, oy, oz in NEIGHBOURS:
-            guarded(exists(ox, oy), lambda ox=ox, oy=oy, oz=oz: fn(halo_copies(k, ox, oy, oz, incoming)))
+    def for_offsets(fn):
+        for ox, oy in OFFSETS:
+            guarded(exists(ox, oy), functools.partial(fn, ox, oy))
+
+    def far_halo(k, fn, incoming=False):
+        for_offsets(lambda ox, oy: fn(halo_copies(k, ox, oy, 1, incoming)))
+
+    def near_halo(k, fn, incoming=False, planes=True):
+        def each(ox, oy):
+            if (ox, oy) == (0, 0):
+                return
+            if planes and oy == 0:
+                fn(plane_copies(k, ox, incoming))
+            fn(halo_copies(k, ox, oy, 0, incoming))
+        for_offsets(each)
+
+    def all_halo(k, fn, incoming=False, planes=True):
+        def each(ox, oy):
+            fn(halo_copies(k, ox, oy, 1, incoming))
+            if (ox, oy) != (0, 0):
+                fn(halo_copies(k, ox, oy, 0, incoming))
+                if planes and oy == 0:
+                    fn(plane_copies(k, ox, incoming))
+        for_offsets(each)
+
+    def for_planes(k, fn):
         for ox in (-1, 1):
-            guarded(exists(ox, 0), lambda ox=ox: fn(plane_copies(k, ox, incoming)))
+            guarded(exists(ox, 0), functools.partial(lambda ox: fn(plane_copies(k, ox, False)), ox))
 
     def info_copies(ox, oy, oz, incoming):
         mine, theirs = oz * 9 + slot_of(ox, oy), oz * 9 + slot_of(-ox, -oy)
         target = device(ox, oy, oz)
+        leaving = coming = pl.ds(0, 8)
+        if oy:
+            leaving, coming = (pl.ds(0, 1), pl.ds(7, 1)) if oy < 0 else (pl.ds(7, 1), pl.ds(0, 1))
+        part = info_send.at[leaving]
         if incoming:
-            return remote(info_send, info_recv.at[oz, slot_of(ox, oy)], info_ss.at[mine], info_rs.at[mine], target)
-        return remote(info_send, info_recv.at[oz, slot_of(-ox, -oy)], info_ss.at[mine], info_rs.at[theirs], target)
+            return remote(part, info_recv.at[oz, slot_of(ox, oy), coming], info_ss.at[mine], info_rs.at[mine], target)
+        return remote(part, info_recv.at[oz, slot_of(-ox, -oy), leaving], info_ss.at[mine], info_rs.at[theirs], target)
 
     def for_info(fn, incoming=False):
-        for ox, oy, oz in NEIGHBOURS:
-            guarded(exists(ox, oy), lambda ox=ox, oy=oy, oz=oz: fn(info_copies(ox, oy, oz, incoming)))
+        def each(ox, oy):
+            fn(info_copies(ox, oy, 1, incoming))
+            if (ox, oy) != (0, 0):
+                fn(info_copies(ox, oy, 0, incoming))
+        for_offsets(each)
 
     def pack_halo(k):
         packed = zero
@@ -400,12 +429,14 @@
                     to = p * 32 + t * 8 + x
                     packed = jnp.where(lane == to, pltpu.roll(v, jnp.where(iz == 0, to + 1, to), 1), packed)
         stage[k, 2] = packed
-        stage[k, 5] = packed
         for p in range(2):
             stage[k, p] = cor[k, p, pl.ds(PY + 8, 8, stride=PY), :]
             stage[k, 3 + p] = cor[k, p, pl.ds(PY + 39, 8, stride=PY), :]
-        lines = [cor[k, p, pl.ds(x * PY + y, 1), :] for p in range(2) for x in (1, 8) for y in (8, 39)]
-        stage[k, 6] = jnp.concatenate(lines, axis=0)
+        for c in range(4):
+            x, y, row = (1, 8)[c // 2], (8, 39)[c % 2], (0, 7)[c % 2]
+            for p in range(2):
+                corners[k, c, pl.ds(p, 1), :] = cor[k, p, pl.ds(x * PY + y, 1), :]
+            corners[k, c, pl.ds(2, 1), :] = packed[row:row + 1]
 
     first_row = pl.ds(0, 1)
     others = pl.ds(0, 16 * nz - 1)
@@ -519,7 +550,7 @@
                 if s == 0 and ox == 0 and oy == 0:
                     tiles[(ox, oy)] = stage[k, 2]
                 elif s == 0 and ox and oy:
-                    tiles[(ox, oy)] = rd[k, corner_of(ox, oy), 0]
+                    tiles[(ox, oy)] = jnp.broadcast_to(rd[k, corner_of(ox, oy), pl.ds(2, 1), :], (8, 128))
                 elif s == 0 and oy:
                     tiles[(ox, oy)] = ry[k, 0, 0] if oy < 0 else ry[k, 1, 2]
                 else:
@@ -556,7 +587,7 @@
         for p in range(2):
             parts = []
             for c in range(4):
-                parts.append(rd[k, c, 1, pl.ds(p * 4 + (3 - c), 1), :])
+                parts.append(rd[k, c, pl.ds(p, 1), :])
             diagonal.append(jnp.concatenate(parts, axis=0))
         pxy = tuple(diagonal)
         for r in range(6):
@@ -639,17 +670,19 @@
             pair_copy(k).start()
             jacobi(k)
             pack_halo(k)
-        for_halo(k, lambda copy: copy.start())
+        far_halo(k, lambda copy: copy.start())
+        near_halo(k, lambda copy: copy.start())
         pair_copy(k).wait_recv()
         gather_start(k)
         if k == 0:
             for_info(lambda copy: copy.wait_recv(), True)
             setup_rounds()
         pair_copy(k).wait_send()
-        for_halo(k, lambda copy: copy.wait_recv(), True)
+        for_planes(k, lambda copy: copy.wait_send())
+        all_halo(k, lambda copy: copy.wait_recv(), True)
         cells = sides_rounds(k)
-        for_halo(k, lambda copy: copy.wait_send())
         main_rounds(k)
+        all_halo(k, lambda copy: copy.wait_send(), planes=False)
         if k == 0:
             for_info(lambda copy: copy.wait_send())
         gather_every(k).wait_recv()
@@ -672,7 +705,7 @@
         block = (CX, CY, CZ)
         return pl.pallas_call(
             functools.partial(kernel, nx, ny),
-            out_shape=jax.ShapeDtypeStruct((2,) + block, F32),
+            out_shape=pltpu.VMEM((2,) + block, F32),
             in_specs=[hbm, hbm, hbm, smem, smem],
             out_specs=vmem,
             scratch_shapes=[
@@ -687,15 +720,15 @@
                 pltpu.VMEM((1024, 128), BF16), pltpu.VMEM((2, 64, 128), F32), pltpu.VMEM((2, 64, 128), F32),
                 pltpu.VMEM((4, 24, 128), F32),
                 pltpu.VMEM(tile, F32), pltpu.VMEM((2, 9) + tile, F32),
-                pltpu.VMEM((SWEEPS, 7) + tile, F32), pltpu.VMEM((SWEEPS, 2, 9) + tile, F32),
-                pltpu.VMEM((SWEEPS, 2, 3) + tile, F32), pltpu.VMEM((SWEEPS, 4, 2) + tile, F32),
+                pltpu.VMEM((SWEEPS, 5) + tile, F32), pltpu.VMEM((SWEEPS, 4) + tile, F32), pltpu.VMEM((SWEEPS, 2, 9) + tile, F32),
+                pltpu.VMEM((SWEEPS, 2, 3) + tile, F32), pltpu.VMEM((SWEEPS, 4) + tile, F32),
                 pltpu.VMEM((SWEEPS,) + tile, F32), pltpu.VMEM((SWEEPS,) + tile, F32), pltpu.VMEM((SWEEPS,) + tile, F32),
                 pltpu.VMEM((SWEEPS, 128, 128), F32),
                 dma((18,)), dma((18,)), dma((SWEEPS, 18)), dma((SWEEPS, 18)),
                 dma((SWEEPS, 2)), dma((SWEEPS, 2)), dma((SWEEPS,)), dma((SWEEPS,)), dma((SWEEPS,)), dma((SWEEPS,)),
             ],
             compiler_params=pltpu.CompilerParams(
-                collective_id=0, has_side_effects=True, vmem_limit_bytes=64 * 1024 * 1024
+                collective_id=0, has_side_effects=True, vmem_limit_bytes=56 * 1024 * 1024
             ),
         )(adjoint_source, velocity, damping, face_rounds, jnp.transpose(aggregates, (0, 2, 1)))
 

time: 45.2 us -> 41.4 us (0.916)
  Pallas kernels: 43.3 us -> 40.5 us
  local copies, waits for them, and re-layouts: 1.67 us -> 0.71 us
    pallas_call x1, Pallas kernels: 43.3 us -> 40.5 us  [step(): pl.pallas_call(functools.partial(kernel, nx, ny), out_shape=pltpu.VMEM((2...]
    unnamed x1, local copies, waits for them, and re-layouts: 1.67 us -> 0.71 us
where the time goes in v2:
time: 41.4 us; the launch traced here: 41.2 us
  Pallas kernels  40.5 us (98%)
  local copies, waits for them, and re-layouts  0.71 us (2%)
    pallas_call x1, Pallas kernels, step(): pl.pallas_call(functools.partial(kernel, nx, ny), out_shape=pltpu.VMEM((2...  40.5 us

profile of v2, /device:TPU:1, one launch (start us, length us, event | category | flops | bytes accessed | tf_op | source)
XLA Modules:
  0.0 41.2 jit_solution(17646963171734916629)
XLA Ops:
  0.0 40.5 %shard_map.55 = f32[2,8,32,128]{3,2,1,0:T(8,128)S(1)} custom-call(f32[2,8,32,128]{3,2,1,0:T(8,128)} %src_in.1, f32[8,32,128]{2,1,0:T(8,128)} %vel_in.1, f32[8,32,128]{2,1,0:T(8,128)} %dmp_in.1, s32[1,1,1,6]{3,2,1,0:T(1,128)} %rounds.1, s32[2,1,4]{2,1,0:T(1,128)} %bitcast.3), custom_call_target="tpu_custom_call" | custom-call | tf_op jit(solution)/shard_map/pallas_call | solution.py:706
  40.5 0.7 %copy.8 = f32[2,8,32,128]{3,2,1,0:T(8,128)} copy(f32[2,8,32,128]{3,2,1,0:T(8,128)S(1)} %shard_map.55) | data formatting | bytes 524288

commit v3 on v2

--- a/solution.py
+++ b/solution.py
@@ -63,7 +63,7 @@
     src_in, vel_in, dmp_in, rounds, aggs, out,
     src, vel, dmp, in_sem,
     kap, kdm, mre, mim, res, ping, pong, cor, fld, fz,
-    coltile, edgecol, onehot, ksum, cval, zmask,
+    coltile, edgecol, onehot, ksum, cval, zmask, coa, coz, own_k,
     info_send, info_recv, stage, corners, rz, ry, rd, row_send, pair_recv, chip_send, gath,
     info_ss, info_rs, h_ss, h_rs, x_ss, x_rs, pair_ss, pair_rs, ga_ss, ga_rs,
 ):
@@ -142,6 +142,11 @@
 
     barrier = pltpu.get_barrier_semaphore()
     count = jnp.int32(16 * nz - 1 + 1)
+    def tell_chip(slot, target):
+        pl.semaphore_signal(barrier, inc=1, device_id=target, device_id_type=MESH)
+
+    for_chips(tell_chip)
+    tell_chip(0, pair)
     for ox, oy in OFFSETS:
         if oy:
             def tell(ox=ox, oy=oy):
@@ -150,11 +155,6 @@
             guarded(exists(ox, oy), tell)
             count = count + jnp.where(exists(ox, oy), 2, 0)
 
-    def tell_chip(slot, target):
-        pl.semaphore_signal(barrier, inc=1, device_id=target, device_id_type=MESH)
-
-    for_chips(tell_chip)
-    tell_chip(0, pair)
 
     for buf in (ping, pong):
         for p in range(2):
@@ -202,7 +202,9 @@
 
     def row_of(sums, first):
         rows = [jnp.sum(sums[p][qx][t], axis=0, keepdims=True) for p in range(2) for qx in range(2) for t in range(TILES)]
-        total = jnp.sum(jnp.concatenate(rows, axis=0), axis=1, keepdims=True)
+        return lanes_of(jnp.sum(jnp.concatenate(rows, axis=0), axis=1, keepdims=True), first)
+
+    def lanes_of(total, first):
         spread = jnp.where(iota(1, (16, 128)) == iota(0, (16, 128)) + first, jnp.broadcast_to(total, (16, 128)), 0.0)
         return jnp.sum(spread, axis=0, keepdims=True)
 
@@ -216,6 +218,11 @@
             sums[0][x // 4][t] = sums[0][x // 4][t] + rows_of(kappa, t)
             sums[1][x // 4][t] = sums[1][x // 4][t] + rows_of(damp, t)
     fixed_row = row_of(sums, 32 + 16 * core)
+    for p in range(2):
+        for qx in range(2):
+            for t in range(TILES):
+                total = jnp.sum(jnp.sum(sums[p][qx][t], axis=0, keepdims=True), axis=1, keepdims=True)
+                own_k[pl.ds(8 * p + TILES * qx + t, 1), :] = jnp.broadcast_to(total, (1, 128))
     for qx in range(2):
         for t in range(TILES):
             fixed_row = fixed_row + jnp.where(lane1 == 64 + 8 * core + qx * TILES + t, ids[qx][t], 0.0)
@@ -241,10 +248,10 @@
     def smooth_z(v):
         return 2.0 * v + jnp.where(first32, 0.0, pltpu.roll(v, 1, 1)) + jnp.where(last32, 0.0, pltpu.roll(v, 127, 1))
 
-    def residual_pass():
+    def residual_pass(field, zone, source):
         lefts = []
         for p in range(2):
-            c0, px, py, pxy = (fz[role, p] for role in range(4))
+            c0, px, py, pxy = (zone[role, p] for role in range(4))
             t0, t3 = (lt == 0) & (sub == 0), (lt == TILES - 1) & (sub == 7)
 
             def smooth_y(v, across):
@@ -265,8 +272,8 @@
         def y_smoothed(p, x):
             if ys[p][x] is None:
                 base = x * PY
-                ys[p][x] = (fld[p, pl.ds(base + 7, 32), :] + fld[p, pl.ds(base + 9, 32), :]
-                            + 2.0 * fld[p, pl.ds(base + 8, 32), :])
+                ys[p][x] = (field[p, pl.ds(base + 7, 32), :] + field[p, pl.ds(base + 9, 32), :]
+                            + 2.0 * field[p, pl.ds(base + 8, 32), :])
             return ys[p][x]
 
         for x in range(CX):
@@ -275,11 +282,11 @@
                 v = y_smoothed(p, x) + 2.0 * y_smoothed(p, x + 1) + y_smoothed(p, x + 2)
                 halo = jnp.concatenate([roll(lefts[p], -(8 * t + x)) for t in range(TILES)], axis=0)
                 smoothed.append(smooth_z(v) + jnp.where(lane32 == zf, halo, 0.0))
-            f_re = fld[0, pl.ds((x + 1) * PY + 8, 32), :]
-            f_im = fld[1, pl.ds((x + 1) * PY + 8, 32), :]
+            f_re = field[0, pl.ds((x + 1) * PY + 8, 32), :]
+            f_im = field[1, pl.ds((x + 1) * PY + 8, 32), :]
             a, b = kap[x], kdm[x]
-            r_re = src[0, x] + 0.25 * smoothed[0] - a * f_re + b * f_im
-            r_im = src[1, x] + 0.25 * smoothed[1] - a * f_im - b * f_re
+            r_re = source[0, x] + 0.25 * smoothed[0] - a * f_re + b * f_im
+            r_im = source[1, x] + 0.25 * smoothed[1] - a * f_im - b * f_re
             res[0, x] = r_re
             res[1, x] = r_im
             for t in range(TILES):
@@ -357,8 +364,9 @@
             part = stage.at[k, 2, leaving]
             there, at_home = rz.at[k, 1, slot_of(-ox, -oy), leaving], rz.at[k, 1, slot_of(ox, oy), coming]
         else:
-            part = stage.at[k, 2]
-            there, at_home = rz.at[k, oz, slot_of(-ox, -oy)], rz.at[k, oz, slot_of(ox, oy)]
+            half = pl.ds(0, 4)
+            part = stage.at[k, 5, half]
+            there, at_home = rz.at[k, oz, slot_of(-ox, -oy), half], rz.at[k, oz, slot_of(ox, oy), half]
         if incoming:
             return remote(part, at_home, h_ss.at[k, mine], h_rs.at[k, mine], target)
         return remote(part, there, h_ss.at[k, mine], h_rs.at[k, theirs], target)
@@ -429,6 +437,7 @@
                     to = p * 32 + t * 8 + x
                     packed = jnp.where(lane == to, pltpu.roll(v, jnp.where(iz == 0, to + 1, to), 1), packed)
         stage[k, 2] = packed
+        stage[k, 5] = jnp.where(lane < 64, packed, roll(packed, 64, 4))
         for p in range(2):
             stage[k, p] = cor[k, p, pl.ds(PY + 8, 8, stride=PY), :]
             stage[k, 3 + p] = cor[k, p, pl.ds(PY + 39, 8, stride=PY), :]
@@ -553,8 +562,11 @@
                     tiles[(ox, oy)] = jnp.broadcast_to(rd[k, corner_of(ox, oy), pl.ds(2, 1), :], (8, 128))
                 elif s == 0 and oy:
                     tiles[(ox, oy)] = ry[k, 0, 0] if oy < 0 else ry[k, 1, 2]
+                elif oy:
+                    tiles[(ox, oy)] = rz[k, s, slot_of(ox, oy)]
                 else:
-                    tiles[(ox, oy)] = rz[k, s, slot_of(ox, oy)]
+                    folded = rz[k, s, slot_of(ox, oy)]
+                    tiles[(ox, oy)] = jnp.where(sub < 4, folded, roll(folded, 64, 4))
             roles = assemble(tiles, 0.0)
             cells.append([(role, roll(role, -32)) for role in roles])
         for r in range(6):
@@ -620,46 +632,83 @@
                 cor[k, p, pl.ds(own_x * PY + halo_y, 1), :] = py[p][c:c + 1]
                 cor[k, p, pl.ds(halo_x * PY + halo_y, 1), :] = pxy[p][c:c + 1]
 
-    def update(k, cells):
+    def add_correction(k, cells):
         last = k == SWEEPS - 1
         for p in range(2):
             turned = [pltpu.roll(cells[0][role][p], zf, 1) for role in range(4)]
-
-            def term(role, t, x):
-                at_qx = (0 if x == 0 else 3) if role % 2 else 1 + x // 4
-                at_qy = (0 if t == 0 else 5) if role // 2 else 1 + t
-                return jnp.broadcast_to(cval[p, pl.ds(at_qx * 6 + at_qy, 1), :], (8, 128))
-
             for x in range(10):
                 if last and x in (0, 9):
                     continue
                 role = 1 if x in (0, 9) else 0
                 near = min(max(x - 1, 0), 7)
                 for t in range(TILES):
-                    value = term(role, t, (near // 4) * 4 if role == 0 else near)
                     column = roll(turned[role], -(8 * t + near))
                     rows = pl.ds(x * PY + 8 + 8 * t, 8)
-                    value = value + fld[p, rows, :] + jnp.where(at_face, column, cor[k, p, rows, :])
-                    if last:
-                        out[p, x - 1, pl.ds(8 * t, 8), :] = value
-                    else:
-                        fld[p, rows, :] = value
+                    fld[p, rows, :] = fld[p, rows, :] + jnp.where(at_face, column, cor[k, p, rows, :])
                 if last:
                     continue
                 for t, at, y in ((0, 0, 7), (TILES - 1, 7, 40)):
                     column = roll(turned[2 + role], -(8 * t + near))[at:at + 1]
                     place = pl.ds(x * PY + y, 1)
-                    value = term(2 + role, t, near)[0:1] + fld[p, place, :]
-                    fld[p, place, :] = value + jnp.where(at_face[0:1], column, cor[k, p, place, :])
+                    fld[p, place, :] = fld[p, place, :] + jnp.where(at_face[0:1], column, cor[k, p, place, :])
+            if not last:
+                for role in range(4):
+                    fz[role, p] = fz[role, p] + cells[1][role][p]
+
+    def term(p, role, t, x, height=8):
+        at_qx = (0 if x == 0 else 3) if role % 2 else 1 + x // 4
+        at_qy = (0 if t == 0 else 5) if role // 2 else 1 + t
+        return jnp.broadcast_to(cval[p, pl.ds(at_qx * 6 + at_qy, 1), :], (height, 128))
+
+    def add_coarse(last):
+        for p in range(2):
+            for x in range(10):
+                if last and x in (0, 9):
+                    continue
+                role = 1 if x in (0, 9) else 0
+                near = min(max(x - 1, 0), 7)
+                for t in range(TILES):
+                    value = term(p, role, t, near)
+                    rows = pl.ds(x * PY + 8 + 8 * t, 8)
+                    if last:
+                        out[p, x - 1, pl.ds(8 * t, 8), :] = fld[p, rows, :] + value
+                    else:
+                        coa[p, rows, :] = value
+                        fld[p, rows, :] = fld[p, rows, :] + value
+                if last:
+                    continue
+                for t, y in ((0, 7), (TILES - 1, 40)):
+                    place = pl.ds(x * PY + y, 1)
+                    value = term(p, 2 + role, t, near, 1)
+                    coa[p, place, :] = value
+                    fld[p, place, :] = fld[p, place, :] + value
             if not last:
                 other = cval[p, pl.ds(24, 24), :]
                 for role in range(4):
                     halo = jnp.broadcast_to(jnp.sum(other * zmask[role], axis=0, keepdims=True), (8, 128))
-                    fz[role, p] = fz[role, p] + cells[1][role][p] + halo
+                    coz[role, p] = halo
+                    fz[role, p] = fz[role, p] + halo
+
+    def coarse_row():
+        values, smooth = [], []
+        for p in range(2):
+            c = cval[p]
+            v = (2.0 * CZ - 1.0) * c[0:24] + 0.5 * c[24:48]
+            for at in (1, 2):
+                u = 7.0 * v[6 * at:6 * at + 6] + 0.5 * (v[6 * at - 6:6 * at] + v[6 * at + 6:6 * at + 12])
+                smooth.append(15.0 * u[1:5] + 0.5 * (u[0:4] + u[2:6]))
+                values.append(c[6 * at + 1:6 * at + 5])
+        c_re, c_im = jnp.concatenate(values[0:2], axis=0), jnp.concatenate(values[2:4], axis=0)
+        s_re, s_im = jnp.concatenate(smooth[0:2], axis=0), jnp.concatenate(smooth[2:4], axis=0)
+        a, b = 16.0 * (4 * 8 * CZ) - own_k[0:8], own_k[8:16]
+        total = jnp.concatenate([a * c_re - b * c_im - 2.0 * s_re, a * c_im + b * c_re - 2.0 * s_im], axis=0)
+        return lanes_of(total, 16 * core)
 
     for k in range(SWEEPS):
-        row = row_of(first_pass() if k == 0 else residual_pass(), 16 * core)
-        row_send[k, first_row] = row + fixed_row if k == 0 else row
+        if k == 0:
+            row_send[k, first_row] = row_of(first_pass(), 16 * core) + fixed_row
+        else:
+            row_send[k, first_row] = row - coarse_row()
         if k == 0:
             jacobi(k)
             pack_halo(k)
@@ -668,28 +717,34 @@
             for_info(lambda copy: copy.start())
         else:
             pair_copy(k).start()
+            add_coarse(False)
+            residual_pass(coa, coz, res)
             jacobi(k)
+            for_planes(k, lambda copy: copy.start())
             pack_halo(k)
         far_halo(k, lambda copy: copy.start())
-        near_halo(k, lambda copy: copy.start())
+        near_halo(k, lambda copy: copy.start(), planes=k == 0)
         pair_copy(k).wait_recv()
         gather_start(k)
         if k == 0:
             for_info(lambda copy: copy.wait_recv(), True)
             setup_rounds()
         pair_copy(k).wait_send()
-        for_planes(k, lambda copy: copy.wait_send())
+        all_halo(k, lambda copy: copy.wait_send())
+        if k == 0:
+            for_info(lambda copy: copy.wait_send())
         all_halo(k, lambda copy: copy.wait_recv(), True)
         cells = sides_rounds(k)
         main_rounds(k)
-        all_halo(k, lambda copy: copy.wait_send(), planes=False)
-        if k == 0:
-            for_info(lambda copy: copy.wait_send())
+        add_correction(k, cells)
+        if k < SWEEPS - 1:
+            row = row_of(residual_pass(fld, fz, src), 16 * core)
         gather_every(k).wait_recv()
         if k == 0:
             setup_aggregates()
         coarse_values(k)
-        update(k, cells)
+        if k == SWEEPS - 1:
+            add_coarse(True)
         gather_every(k).wait_send()
 
 
@@ -718,9 +773,10 @@
                 pltpu.VMEM((4, 2) + tile, F32),
                 pltpu.VMEM((12,) + tile, F32), pltpu.VMEM((4, 4, 128), F32),
                 pltpu.VMEM((1024, 128), BF16), pltpu.VMEM((2, 64, 128), F32), pltpu.VMEM((2, 64, 128), F32),
-                pltpu.VMEM((4, 24, 128), F32),
+                pltpu.VMEM((4, 24, 128), F32), pltpu.VMEM((2, 10 * PY, CZ), F32), pltpu.VMEM((4, 2) + tile, F32),
+                pltpu.VMEM((16, 128), F32),
                 pltpu.VMEM(tile, F32), pltpu.VMEM((2, 9) + tile, F32),
-                pltpu.VMEM((SWEEPS, 5) + tile, F32), pltpu.VMEM((SWEEPS, 4) + tile, F32), pltpu.VMEM((SWEEPS, 2, 9) + tile, F32),
+                pltpu.VMEM((SWEEPS, 6) + tile, F32), pltpu.VMEM((SWEEPS, 4) + tile, F32), pltpu.VMEM((SWEEPS, 2, 9) + tile, F32),
                 pltpu.VMEM((SWEEPS, 2, 3) + tile, F32), pltpu.VMEM((SWEEPS, 4) + tile, F32),
                 pltpu.VMEM((SWEEPS,) + tile, F32), pltpu.VMEM((SWEEPS,) + tile, F32), pltpu.VMEM((SWEEPS,) + tile, F32),
                 pltpu.VMEM((SWEEPS, 128, 128), F32),

time: 41.4 us -> 40.2 us (0.971)
  Pallas kernels: 40.5 us -> 39.4 us
    pallas_call x1, Pallas kernels: 40.5 us -> 39.4 us  [step(): pl.pallas_call(functools.partial(kernel, nx, ny), out_shape=pltpu.VMEM((2...]
where the time goes in v3:
time: 40.2 us
  Pallas kernels  39.4 us (98%)
  local copies, waits for them, and re-layouts  0.71 us (2%)
    pallas_call x1, Pallas kernels, step(): pl.pallas_call(functools.partial(kernel, nx, ny), out_shape=pltpu.VMEM((2...  39.4 us

profile of v3, /device:TPU:1, one launch (start us, length us, event | category | flops | bytes accessed | tf_op | source)
XLA Modules:
  0.0 40.2 jit_solution(4100369276475912435)
XLA Ops:
  0.0 39.4 %shard_map.55 = f32[2,8,32,128]{3,2,1,0:T(8,128)S(1)} custom-call(f32[2,8,32,128]{3,2,1,0:T(8,128)} %src_in.1, f32[8,32,128]{2,1,0:T(8,128)} %vel_in.1, f32[8,32,128]{2,1,0:T(8,128)} %dmp_in.1, s32[1,1,1,6]{3,2,1,0:T(1,128)} %rounds.1, s32[2,1,4]{2,1,0:T(1,128)} %bitcast.3), custom_call_target="tpu_custom_call" | custom-call | tf_op jit(solution)/shard_map/pallas_call | solution.py:761
  39.4 0.7 %copy.8 = f32[2,8,32,128]{3,2,1,0:T(8,128)} copy(f32[2,8,32,128]{3,2,1,0:T(8,128)S(1)} %shard_map.55) | data formatting | bytes 524288

commit v4 on v3

--- a/solution.py
+++ b/solution.py
@@ -104,7 +104,7 @@
     across = sorted(((dx, dy) for dx in range(4) for dy in range(4)), key=lambda d: -min(d[0], 4 - d[0]) - min(d[1], 4 - d[1]))
     across_x = [lax.rem(at_y + dy, 4) * 4 + lax.rem(at_x + dx, 4) for dx, dy in across]
 
-    def for_chips(fn):
+    def for_chips(fn, first=0, last=nz - 1, rest=True):
         def layer(i, carry):
             step = (i + 1) // 2
             there = lax.rem(at_z + nz // 2 + jnp.where(lax.rem(i, 2) == 1, nz - step, step), nz)
@@ -112,8 +112,8 @@
             for j in range(16):
                 fn(i * 16 + j, (across_x[j], ty, tz))
             return carry
-        lax.fori_loop(0, nz - 1, layer, 0)
-        for j in range(15):
+        lax.fori_loop(first, last, layer, 0)
+        for j in range(15 if rest else 0):
             fn((nz - 1) * 16 + j, (across_x[j], iy, iz))
 
     loads = [pltpu.make_async_copy(whole, local, in_sem.at[i])
@@ -453,12 +453,15 @@
     def pair_copy(k):
         return remote(row_send.at[k, first_row], pair_recv.at[k, first_row], pair_ss.at[k], pair_rs.at[k], pair)
 
-    def gather_start(k):
+    def chip_row(k):
+        pair_copy(k).wait_recv()
         chip = row_send[k, first_row] + pair_recv[k, first_row]
         chip_send[k, first_row] = chip
         gath[k, pl.ds(16 * nz - 1, 1)] = chip
+
+    def gather_start(k, *layers):
         for_chips(lambda slot, target: remote(
-            chip_send.at[k, first_row], gath.at[k, pl.ds(slot, 1)], ga_ss.at[k], ga_rs.at[k], target).start())
+            chip_send.at[k, first_row], gath.at[k, pl.ds(slot, 1)], ga_ss.at[k], ga_rs.at[k], target).start(), *layers)
 
     def gather_every(k):
         return remote(gath.at[k, others], gath.at[k, others], ga_ss.at[k], ga_rs.at[k], pair)
@@ -719,13 +722,16 @@
             pair_copy(k).start()
             add_coarse(False)
             residual_pass(coa, coz, res)
+            chip_row(k)
+            gather_start(k, 0, 1, False)
             jacobi(k)
             for_planes(k, lambda copy: copy.start())
             pack_halo(k)
         far_halo(k, lambda copy: copy.start())
         near_halo(k, lambda copy: copy.start(), planes=k == 0)
-        pair_copy(k).wait_recv()
-        gather_start(k)
+        if k == 0:
+            chip_row(k)
+        gather_start(k, 0 if k == 0 else 1)
         if k == 0:
             for_info(lambda copy: copy.wait_recv(), True)
             setup_rounds()

time: 40.2 us -> 42 us (1.045)
  Pallas kernels: 39.4 us -> 41.2 us
    pallas_call x1, Pallas kernels: 39.4 us -> 41.2 us  [step(): pl.pallas_call(functools.partial(kernel, nx, ny), out_shape=pltpu.VMEM((2...]
where the time goes in v4:
time: 42 us; the launch traced here: 41.9 us
  Pallas kernels  41.2 us (98%)
  local copies, waits for them, and re-layouts  0.71 us (2%)
    pallas_call x1, Pallas kernels, step(): pl.pallas_call(functools.partial(kernel, nx, ny), out_shape=pltpu.VMEM((2...  41.2 us

profile of v4, /device:TPU:1, one launch (start us, length us, event | category | flops | bytes accessed | tf_op | source)
XLA Modules:
  0.0 41.9 jit_solution(11410176030985107434)
XLA Ops:
  0.0 41.2 %shard_map.55 = f32[2,8,32,128]{3,2,1,0:T(8,128)S(1)} custom-call(f32[2,8,32,128]{3,2,1,0:T(8,128)} %src_in.1, f32[8,32,128]{2,1,0:T(8,128)} %vel_in.1, f32[8,32,128]{2,1,0:T(8,128)} %dmp_in.1, s32[1,1,1,6]{3,2,1,0:T(1,128)} %rounds.1, s32[2,1,4]{2,1,0:T(1,128)} %bitcast.3), custom_call_target="tpu_custom_call" | custom-call | tf_op jit(solution)/shard_map/pallas_call | solution.py:767
  41.2 0.7 %copy.8 = f32[2,8,32,128]{3,2,1,0:T(8,128)} copy(f32[2,8,32,128]{3,2,1,0:T(8,128)S(1)} %shard_map.55) | data formatting | bytes 524288

commit v5 on v3

--- a/solution.py
+++ b/solution.py
@@ -248,7 +248,7 @@
     def smooth_z(v):
         return 2.0 * v + jnp.where(first32, 0.0, pltpu.roll(v, 1, 1)) + jnp.where(last32, 0.0, pltpu.roll(v, 127, 1))
 
-    def residual_pass(field, zone, source):
+    def residual_pass(field, zone, source, flat=False):
         lefts = []
         for p in range(2):
             c0, px, py, pxy = (zone[role, p] for role in range(4))
@@ -281,7 +281,8 @@
             for p in range(2):
                 v = y_smoothed(p, x) + 2.0 * y_smoothed(p, x + 1) + y_smoothed(p, x + 2)
                 halo = jnp.concatenate([roll(lefts[p], -(8 * t + x)) for t in range(TILES)], axis=0)
-                smoothed.append(smooth_z(v) + jnp.where(lane32 == zf, halo, 0.0))
+                along = 4.0 * v - jnp.where(first32 | last32, v, 0.0) if flat else smooth_z(v)
+                smoothed.append(along + jnp.where(lane32 == zf, halo, 0.0))
             f_re = field[0, pl.ds((x + 1) * PY + 8, 32), :]
             f_im = field[1, pl.ds((x + 1) * PY + 8, 32), :]
             a, b = kap[x], kdm[x]
@@ -674,20 +675,26 @@
                         out[p, x - 1, pl.ds(8 * t, 8), :] = fld[p, rows, :] + value
                     else:
                         coa[p, rows, :] = value
-                        fld[p, rows, :] = fld[p, rows, :] + value
                 if last:
                     continue
                 for t, y in ((0, 7), (TILES - 1, 40)):
                     place = pl.ds(x * PY + y, 1)
                     value = term(p, 2 + role, t, near, 1)
                     coa[p, place, :] = value
-                    fld[p, place, :] = fld[p, place, :] + value
             if not last:
                 other = cval[p, pl.ds(24, 24), :]
                 for role in range(4):
                     halo = jnp.broadcast_to(jnp.sum(other * zmask[role], axis=0, keepdims=True), (8, 128))
                     coz[role, p] = halo
-                    fz[role, p] = fz[role, p] + halo
+
+    def keep_coarse():
+        for p in range(2):
+            for x in range(10):
+                for y, height in ((7, 1), (8, 32), (40, 1)):
+                    rows = pl.ds(x * PY + y, height)
+                    fld[p, rows, :] = fld[p, rows, :] + coa[p, rows, :]
+            for role in range(4):
+                fz[role, p] = fz[role, p] + coz[role, p]
 
     def coarse_row():
         values, smooth = [], []
@@ -718,7 +725,7 @@
         else:
             pair_copy(k).start()
             add_coarse(False)
-            residual_pass(coa, coz, res)
+            residual_pass(coa, coz, res, flat=True)
             jacobi(k)
             for_planes(k, lambda copy: copy.start())
             pack_halo(k)
@@ -729,6 +736,8 @@
         if k == 0:
             for_info(lambda copy: copy.wait_recv(), True)
             setup_rounds()
+        if k > 0:
+            keep_coarse()
         pair_copy(k).wait_send()
         all_halo(k, lambda copy: copy.wait_send())
         if k == 0:

time: 40.2 us -> 40.3 us (level)
  no operation moved by 1% of the time
where the time goes in v5:
time: 40.3 us; the launch traced here: 40.2 us
  Pallas kernels  39.5 us (98%)
  local copies, waits for them, and re-layouts  0.71 us (2%)
    pallas_call x1, Pallas kernels, step(): pl.pallas_call(functools.partial(kernel, nx, ny), out_shape=pltpu.VMEM((2...  39.5 us

profile of v5, /device:TPU:1, one launch (start us, length us, event | category | flops | bytes accessed | tf_op | source)
XLA Modules:
  0.0 40.2 jit_solution(15866136951973173314)
XLA Ops:
  0.0 39.5 %shard_map.55 = f32[2,8,32,128]{3,2,1,0:T(8,128)S(1)} custom-call(f32[2,8,32,128]{3,2,1,0:T(8,128)} %src_in.1, f32[8,32,128]{2,1,0:T(8,128)} %vel_in.1, f32[8,32,128]{2,1,0:T(8,128)} %dmp_in.1, s32[1,1,1,6]{3,2,1,0:T(1,128)} %rounds.1, s32[2,1,4]{2,1,0:T(1,128)} %bitcast.3), custom_call_target="tpu_custom_call" | custom-call | tf_op jit(solution)/shard_map/pallas_call | solution.py:770
  39.5 0.7 %copy.8 = f32[2,8,32,128]{3,2,1,0:T(8,128)} copy(f32[2,8,32,128]{3,2,1,0:T(8,128)S(1)} %shard_map.55) | data formatting | bytes 524288
